TPU v7x, 32 devices: a whole 2x2x4 slice. The times are simulated.
32 devices in a mesh: sector: 2 (over y), rd: 4 (over x, core), pr: 4 (over z).
Axes of the slice: x: 2, y: 2, z: 4, core: 2. Of those that a mesh axis runs over, the one named last changes fastest.
Arguments:
- reading_geo: float32 [3, 131072], P(None, ('sector', 'rd')), parts along dimension 1, may hold values from 0 to 10, as said below
- prism_geo: float32 [3, 524288], P(None, ('sector', 'pr')), parts along dimension 1, may hold values from 0 to 10, as said below
- observed: float32 [131072], P(('sector', 'rd', 'pr')), parts along dimension 0, may hold values from -6 to 6
- warm_start: float32 [524288], P(('sector', 'pr', 'rd')), parts along dimension 0, may hold values from -6 to 6
- damping: float32 [524288], P(('sector', 'pr', 'rd')), parts along dimension 0, may hold values from 0.1 to 2
- pair_blocks: int32 [8, 4, 20, 2], P(('sector', 'rd'), 'pr'), parts along dimension 0, may hold values from 0 to 127, as said below
- pair_count: int32 [8, 4], P(('sector', 'rd'), 'pr'), parts along dimension 0, may hold values from 1 to 20, as said below
Outputs:
- solution: float32 [524288], P(('sector', 'pr', 'rd')), parts along dimension 0
- normal_residual: float32 [524288], P(('sector', 'pr', 'rd')), parts along dimension 0
There are 2 independent parts, one for each index of `sector`. A program takes and returns all parts, laid end to end along the dimension named above; each array names one. Nothing has to cross between parts.
Inputs may be any that keep to these rules, and one draw needn't show every extreme that they name: `pair_blocks`: column 0 is a reading block of the device's rd row (0 to 31), column 1 a prism block of its pr column (0 to 127); the used slots of one device name distinct pairs; slots at or beyond pair_count are ignored. Taking the prism blocks in aligned runs of 32, the slots of one device name at most 2 distinct prism blocks of any one run, and the first 2 slots of every device name 2 distinct blocks of one run. `pair_count`: one device of the sector uses all 20 slots. `reading_geo`: Rows: east and north within 0 to 10, height 0.3 to 0.6. `prism_geo`: Rows: east and north within 0 to 10, depth 1 to 2.
All inputs are finite; a program needn't handle non-finite values.
Results may differ from a plain program's by a relative error of at most 0.0003.
Values sent between devices are 32-bit elements; how exact they have to be, the bound alone decides.
No kernel may reach another device: no remote copies, remote signals or barrier semaphores. Data moves between devices by JAX's collectives and lax.ppermute only.
A program may use at most 64 MiB of HBM per device.

v0:
```python
import functools

import jax
import jax.numpy as jnp
from jax import lax
from jax.experimental import pallas as pl
from jax.experimental.pallas import tpu as pltpu
from jax.sharding import PartitionSpec as P

BLK = 512
LANES = 128
ROWS = BLK // LANES
GROUPS = BLK // 8
SLOTS = 2
MIB = 1024 * 1024
FEATURES = 64

length_scale = 8.0**0.5

F32 = jnp.float32
BF16 = jnp.bfloat16
I32 = jnp.int32
VMEM = pltpu.VMEM
SMEM = pltpu.SMEM


def call(kernel, name, room, outs, ins, args, scratch=()):
    return pl.pallas_call(
        kernel,
        name=name,
        out_shape=outs,
        in_specs=[pl.BlockSpec(memory_space=s) for s in ins],
        out_specs=[pl.BlockSpec(memory_space=getattr(o, "memory_space", VMEM)) for o in outs],
        scratch_shapes=scratch,
        compiler_params=pltpu.CompilerParams(vmem_limit_bytes=room * MIB),
    )(*args)


def lane_index(shape):
    return lax.broadcasted_iota(jnp.int32, shape, len(shape) - 1)


def each(count, one):
    lax.fori_loop(0, count, lambda i, carry: (one(i), carry)[1], 0)


def over(n, one, carry=0):
    if n > 8:
        return lax.fori_loop(0, n, one, carry)
    for s in range(n):
        carry = one(s, carry)
    return carry


def split3(x):
    a = x.astype(BF16).astype(F32)
    b = (x - a).astype(BF16).astype(F32)
    return a, b, x - a - b


def total(values):
    return jnp.sum(jnp.sum(values, axis=0), keepdims=True)


def prep_kernel(pairs, count, place, x0, damp, payload, table, ids, info, sems):
    own = x0.shape[0]
    slots = ids.shape[0]
    copies = [
        pltpu.make_async_copy(x0, payload.at[pl.ds(0, own)], sems.at[0]),
        pltpu.make_async_copy(damp, payload.at[pl.ds(own, own)], sems.at[1]),
    ]
    for copy in copies:
        copy.start()
    for s in range(slots):
        ids[s] = -1
    info[0] = place[0]
    info[1] = place[1]
    info[2] = count[0, 0]

    def assign(i, carry):
        block = pairs[1, i]
        share = block // own
        held = ids[share * SLOTS]
        here = jnp.logical_or(held < 0, held == block)
        slot = share * SLOTS + jnp.where(here, 0, 1)
        ids[slot] = block
        table[0, i] = pairs[0, i]
        table[1, i] = slot
        return carry

    lax.fori_loop(0, count[0, 0], assign, 0)
    payload[2 * own] = scalar_tile([ids[s].astype(F32) for s in range(slots)])
    for copy in copies:
        copy.wait()


def scaled(geo):
    row = lax.broadcasted_iota(I32, geo.shape, 0)
    return (geo - jnp.where(row < 2, 5.0, 0.0)) * length_scale


def features(geo, reading):
    row = lax.broadcasted_iota(I32, geo.shape, 0)
    norm = split3(jnp.broadcast_to(jnp.sum(geo * geo, axis=0, keepdims=True), geo.shape))
    last = jnp.where(row < 6, 1.0, 0.0)
    for k in range(3):
        last = jnp.where(row == (k if reading else 3 + k), norm[k], last)
    if reading:
        a, b, c = split3(geo * jnp.where(row < 2, -2.0, 2.0))
        blocks = [a, a, b, b, a, c, last]
    else:
        a, b, c = split3(geo)
        blocks = [a, b, a, b, c, a, last]
    blocks += [jnp.zeros_like(geo)] * (FEATURES // 8 - len(blocks))
    return jnp.concatenate(blocks, axis=0).astype(BF16)


def tiles_kernel(table, ids, info, readings, prisms, tiles, rgeo, pgeo, depth, feats, rsems, psems):
    slots = ids.shape[0]
    count = info[2]

    def reading_copy(i):
        start = pl.multiple_of(table[0, i] * BLK, BLK)
        return pltpu.make_async_copy(readings.at[:, pl.ds(start, BLK)], rgeo.at[i, pl.ds(0, 3)], rsems.at[i])

    def prism_copy(s):
        start = pl.multiple_of(jnp.maximum(ids[s], 0) * BLK, BLK)
        return pltpu.make_async_copy(prisms.at[:, pl.ds(start, BLK)], pgeo.at[s, pl.ds(0, 3)], psems.at[s])

    rgeo[...] = jnp.zeros(rgeo.shape, F32)
    pgeo[...] = jnp.zeros(pgeo.shape, F32)
    for s in range(slots):
        prism_copy(s).start()
    lax.fori_loop(0, count, lambda i, c: (reading_copy(i).start(), c)[1], 0)

    def prepare(s, carry):
        prism_copy(s).wait()
        geo = scaled(pgeo[s])
        feats[s] = features(geo, False).astype(F32)
        for q in range(ROWS):
            turned = geo[:, q * LANES : (q + 1) * LANES].T
            for g in range(GROUPS // ROWS):
                depth[s * GROUPS + q * (GROUPS // ROWS) + g] = jnp.broadcast_to(
                    turned[8 * g : 8 * g + 8, 2:3], (8, LANES)
                )
        return carry

    over(slots, prepare)
    lax.fori_loop(0, count, lambda i, c: (reading_copy(i).wait(), c)[1], 0)

    def one(i):
        s = table[1, i]
        geo = scaled(rgeo[i])
        mine = features(geo, True)
        theirs = feats[s].astype(BF16)
        tile = tiles.at[pl.ds(i * GROUPS, GROUPS)]
        depths = depth.at[pl.ds(s * GROUPS, GROUPS)]
        height = [jnp.broadcast_to(geo[2:3, c * LANES : (c + 1) * LANES], (8, LANES)) for c in range(ROWS)]
        for q in range(ROWS):
            squared = lax.dot_general(
                theirs[:, q * LANES : (q + 1) * LANES], mine, (((0,), (0,)), ((), ())), preferred_element_type=F32
            )
            for g in range(GROUPS // ROWS):
                v = q * (GROUPS // ROWS) + g
                up = depths[v]
                for c in range(ROWS):
                    w = height[c] + up
                    inv = lax.rsqrt(squared[8 * g : 8 * g + 8, c * LANES : (c + 1) * LANES])
                    tile[v, :, c * LANES : (c + 1) * LANES] = (w * inv) * (inv * inv)

    def two(i, carry):
        one(2 * i)
        one(jnp.minimum(2 * i + 1, count - 1))
        return carry

    lax.fori_loop(0, (count + 1) // 2, two, 0)


def spread_lanes(need, spread):
    slots = need.shape[0]
    values = need[...].reshape(slots * ROWS, LANES)
    left = jnp.concatenate(split3(values), axis=0).astype(BF16)
    shape = (3 * slots * ROWS, ROWS * LANES)
    row = lax.broadcasted_iota(I32, shape, 0) % (slots * ROWS)
    part = lax.broadcasted_iota(I32, shape, 1) // LANES

    def one(s, carry):
        pick = jnp.where(row == ROWS * s + part, 1.0, 0.0).astype(BF16)
        got = lax.dot_general(left, pick, (((0,), (0,)), ((), ())), preferred_element_type=F32)
        for q in range(ROWS):
            for g in range(GROUPS // ROWS):
                spread[s * GROUPS + q * (GROUPS // ROWS) + g] = got[8 * g : 8 * g + 8, q * LANES : (q + 1) * LANES]
        return carry

    over(slots, one)


def forward_tiles(table, count, tiles, need, spread, out):
    spread_lanes(need, spread)

    def one(i):
        a = table[0, i]
        s = table[1, i]
        tile = tiles.at[pl.ds(i * GROUPS, GROUPS)]
        column = spread.at[pl.ds(s * GROUPS, GROUPS)]
        sums = [[jnp.zeros((8, LANES), F32) for _ in range(ROWS)] for _ in range(2)]
        for v in range(GROUPS):
            values = column[v]
            for c in range(ROWS):
                sums[v % 2][c] += tile[v, :, c * LANES : (c + 1) * LANES] * values
        added = [jnp.sum(sums[0][c] + sums[1][c], axis=0, keepdims=True) for c in range(ROWS)]
        out[a] += jnp.concatenate(added, axis=0)

    each(count, one)


def adjoint_tiles(table, count, tiles, row, wide, out):
    slots = wide.shape[0] // GROUPS
    wide[...] = jnp.zeros(wide.shape, F32)

    def one(i):
        s = table[1, i]
        values = row[table[0, i]]
        spread = [jnp.broadcast_to(values[c : c + 1], (8, LANES)) for c in range(ROWS)]
        tile = tiles.at[pl.ds(i * GROUPS, GROUPS)]
        held = wide.at[pl.ds(s * GROUPS, GROUPS)]
        for v in range(GROUPS):
            t = [tile[v, :, c * LANES : (c + 1) * LANES] * spread[c] for c in range(ROWS)]
            held[v] += (t[0] + t[1]) + (t[2] + t[3])

    each(count, one)
    lane = lane_index((8, LANES))

    def reduce(s, groups):
        groups = list(groups)
        for g in range(GROUPS // ROWS):
            for q in range(ROWS):
                added = jnp.sum(wide[s * GROUPS + q * (GROUPS // ROWS) + g], axis=1, keepdims=True)
                groups[g] = jnp.where(lane == ROWS * s + q, added, groups[g])
        return tuple(groups)

    groups = over(slots, reduce, (jnp.zeros((8, LANES), F32),) * (GROUPS // ROWS))
    flat = jnp.concatenate(groups, axis=0).T
    out[0:slots] = flat[0 : slots * ROWS].reshape(slots, ROWS, LANES)


def scalar_tile(values):
    lane = lane_index((ROWS, LANES))
    row = lax.broadcasted_iota(I32, (ROWS, LANES), 0)
    tile = jnp.zeros((ROWS, LANES), F32)
    for k, value in enumerate(values):
        tile = jnp.where(jnp.logical_and(lane == k, row == 0), value, tile)
    return tile


def first_forward_kernel(n_rd, *refs):
    table, ids, info, obs, tiles = refs[:5]
    sent = refs[5 : 5 + n_rd]
    out, x0n, dampn, names, spread, tags, sems = refs[5 + n_rd :]
    slots = ids.shape[0]
    own = (sent[0].shape[0] - 1) // 2
    me = info[0]
    for k in range(n_rd):
        tags[k] = sent[k][2 * own].astype(I32)
    copy = pltpu.make_async_copy(tags, names, sems.at[0])
    copy.start()
    for k in range(n_rd):
        share = partner(me, k, n_rd)
        for j in range(SLOTS):
            slot = share * SLOTS + j
            local = jnp.maximum(ids[slot] - share * own, 0)
            x0n[slot] = sent[k][local]
            dampn[slot] = sent[k][own + local]
    out[...] = jnp.zeros(out.shape, F32)
    forward_tiles(table, info[2], tiles, x0n, spread, out)
    out[...] = -out[...]
    mine = obs.shape[0]
    start = info[1] * mine
    out[pl.ds(start, mine)] = out[pl.ds(start, mine)] + obs[...]
    copy.wait()


def row_kernel(n_pr, stage, *refs):
    table, info, tiles = refs[:3]
    shares = refs[3 : 3 + n_pr]
    rest = refs[3 + n_pr :]
    if stage == 2:
        image0, rest = rest[0], rest[1:]
    payload, image, wide = rest
    blocks = image.shape[0]
    slots = payload.shape[0] - 1
    summed = shares[0][0:blocks]
    for share in shares[1:]:
        summed = summed + share[0:blocks]
    image[...] = summed
    if stage > 0:
        scalars = shares[0][blocks]
        for share in shares[1:]:
            scalars = scalars + share[blocks]
        added = [0.0, total(summed * summed)]
        if stage == 2:
            added.append(total(summed * image0[...]))
        payload[slots] = scalars + scalar_tile(added)
    else:
        payload[slots] = jnp.zeros((ROWS, LANES), F32)
    adjoint_tiles(table, info[2], tiles, image, wide, payload)


def own_sums(me, names, sent, own, into):
    into[...] = jnp.zeros(into.shape, F32)
    for k in range(len(sent)):
        for j in range(SLOTS):
            slot = me * SLOTS + j
            local = jnp.maximum(names[k, 0, slot] - me * own, 0)
            into[local] += sent[k][slot]


def needed_sums(names, sent, slots):
    found = []
    for s in range(slots):
        tag = names[0, 0, s]
        value = sent[0][s]
        for k in range(1, len(sent)):
            for j in range(SLOTS):
                other = s // SLOTS * SLOTS + j
                value = value + jnp.where(names[k, 0, other] == tag, sent[k][other], 0.0)
        found.append(value)
    return jnp.stack(found)


def second_forward_kernel(n_rd, *refs):
    table, info, names, tiles, x0, damp, x0n, dampn = refs[:8]
    sent = refs[8 : 8 + n_rd]
    out, res, resn, spread = refs[8 + n_rd :]
    blocks = out.shape[0] - 1
    own = x0.shape[0]
    own_sums(info[0], names, sent, own, res)
    r = res[...] - damp[...] * x0[...]
    res[...] = r
    resn[...] = needed_sums(names, sent, resn.shape[0]) - dampn[...] * x0n[...]
    out[...] = jnp.zeros(out.shape, F32)
    out[blocks] = scalar_tile([total(r * r), total(damp[...] * r * r)])
    forward_tiles(table, info[2], tiles, resn, spread, out)


def column_scalars(sent, slots, many):
    summed = sent[0][slots]
    for other in sent[1:]:
        summed = summed + other[slots]
    return [summed[0:1, k : k + 1] for k in range(many)]


def third_forward_kernel(n_rd, *refs):
    table, info, names, tiles, x0, damp, dampn, res0, res0n = refs[:9]
    sent = refs[9 : 9 + n_rd]
    out, x1, res1, prod0, known, res1n, spread = refs[9 + n_rd :]
    blocks = out.shape[0] - 1
    slots = res0n.shape[0]
    own = x0.shape[0]
    r0 = res0[...]
    own_sums(info[0], names, sent, own, prod0)
    q0 = prod0[...] + damp[...] * r0
    norm, bending = column_scalars(sent, slots, 2)
    step = norm / bending
    prod0[...] = q0
    x1[...] = x0[...] + step * r0
    r1 = r0 - step * q0
    res1[...] = r1
    res1n[...] = res0n[...] - step * (needed_sums(names, sent, slots) + dampn[...] * res0n[...])
    known[0] = scalar_tile([norm, bending])
    out[...] = jnp.zeros(out.shape, F32)
    out[blocks] = scalar_tile([total(r1 * r1), total(damp[...] * r1 * r1), total(damp[...] * r1 * r0)])
    forward_tiles(table, info[2], tiles, res1n, spread, out)


def last_kernel(n_rd, *refs):
    info, names, damp, x1, res0, res1, prod0, known = refs[:8]
    sent = refs[8 : 8 + n_rd]
    x2, res2, sums = refs[8 + n_rd :]
    own = damp.shape[0]
    slots = sent[0].shape[0] - 1
    r1 = res1[...]
    own_sums(info[0], names, sent, own, sums)
    h1 = sums[...] + damp[...] * r1
    norm1, r1_a_r1, r1_a_r0 = column_scalars(sent, slots, 3)
    norm0 = known[0][0:1, 0:1]
    bending0 = known[0][0:1, 1:2]
    ratio = norm1 / norm0
    bending = r1_a_r1 + ratio * (2.0 * r1_a_r0 + ratio * bending0)
    step = norm1 / bending
    x2[...] = x1[...] + step * (r1 + ratio * res0[...])
    res2[...] = r1 - step * (h1 + ratio * prod0[...])


def partner(me, k, n):
    if n & (n - 1) == 0:
        return me ^ k
    return lax.rem(me + n - k, n)


def exchange(values, axis, n):
    got = [values]
    for k in range(1, n):
        if n & (n - 1) == 0:
            pairs = [(i, i ^ k) for i in range(n)]
        else:
            pairs = [(i, (i + k) % n) for i in range(n)]
        got.append(lax.ppermute(values, axis, pairs))
    return got


def body(n_rd, n_pr, reading_geo, prism_geo, observed, warm_start, damping, pair_blocks, pair_count):
    cap = pair_blocks.shape[2]
    pairs = pair_blocks.reshape(cap, 2).T
    own = warm_start.shape[0] // BLK
    rblk = reading_geo.shape[1] // BLK
    slots = n_rd * SLOTS
    shaped = lambda v: v.reshape(-1, ROWS, LANES)
    x0, damp, obs = shaped(warm_start), shaped(damping), shaped(observed)
    place = jnp.stack([lax.axis_index("rd"), lax.axis_index("pr")]).astype(I32)
    array = lambda *lead: VMEM((*lead, ROWS, LANES), F32)
    wide = VMEM((slots * GROUPS, 8, LANES), F32)
    dma = pltpu.SemaphoreType.DMA
    room = 5 + slots * GROUPS * 8 * LANES * 4 // MIB

    payload, table, ids, info = call(
        prep_kernel,
        "prep",
        room,
        [array(2 * own + 1), SMEM((2, cap), I32), SMEM((slots,), I32), SMEM((3,), I32)],
        [SMEM, SMEM, SMEM, pl.ANY, pl.ANY],
        [pairs, pair_count, place, x0, damp],
        [dma((2,))],
    )
    columns = exchange(payload, "rd", n_rd)
    (tiles,) = call(
        tiles_kernel,
        "tiles",
        room + slots * FEATURES * BLK * 4 // MIB,
        [VMEM((cap * GROUPS, 8, BLK), F32)],
        [SMEM, SMEM, SMEM, pl.ANY, pl.ANY],
        [table, ids, info, reading_geo, prism_geo],
        [
            VMEM((cap, 8, BLK), F32),
            VMEM((slots, 8, BLK), F32),
            wide,
            VMEM((slots, FEATURES, BLK), F32),
            dma((cap,)),
            dma((slots,)),
        ],
    )
    share, x0n, dampn, names = call(
        functools.partial(first_forward_kernel, n_rd),
        "first_forward",
        room,
        [array(rblk), array(slots), array(slots), SMEM((n_rd, ROWS, LANES), I32)],
        [SMEM] * 3 + [VMEM] * (2 + n_rd),
        [table, ids, info, obs, tiles, *columns],
        [wide, VMEM((n_rd, ROWS, LANES), I32), dma((1,))],
    )
    rows = exchange(share, "pr", n_pr)

    def row_stage(stage, rows, extra):
        keep = stage == 1
        return call(
            functools.partial(row_kernel, n_pr, stage),
            f"row_{stage}",
            room,
            [array(slots + 1)] + [array(rblk)] * keep,
            [SMEM] * 2 + [VMEM] * (1 + n_pr + len(extra)),
            [table, info, tiles, *rows, *extra],
            [array(rblk)] * (not keep) + [wide],
        )

    (sums,) = row_stage(0, rows, [])
    columns = exchange(sums, "rd", n_rd)
    share, res0, res0n = call(
        functools.partial(second_forward_kernel, n_rd),
        "second_forward",
        room,
        [array(rblk + 1), array(own), array(slots)],
        [SMEM] * 3 + [VMEM] * (5 + n_rd),
        [table, info, names, tiles, x0, damp, x0n, dampn, *columns],
        [wide],
    )
    rows = exchange(share, "pr", n_pr)
    sums, image0 = row_stage(1, rows, [])
    columns = exchange(sums, "rd", n_rd)
    share, x1, res1, prod0, known = call(
        functools.partial(third_forward_kernel, n_rd),
        "third_forward",
        room,
        [array(rblk + 1), array(own), array(own), array(own), array(1)],
        [SMEM] * 3 + [VMEM] * (6 + n_rd),
        [table, info, names, tiles, x0, damp, dampn, res0, res0n, *columns],
        [array(slots), wide],
    )
    rows = exchange(share, "pr", n_pr)
    (sums,) = row_stage(2, rows, [image0])
    columns = exchange(sums, "rd", n_rd)
    result = jax.ShapeDtypeStruct((own, ROWS, LANES), F32)
    x2, res2 = call(
        functools.partial(last_kernel, n_rd),
        "last",
        room,
        [result, result],
        [SMEM] * 2 + [VMEM] * (6 + n_rd),
        [info, names, damp, x1, res0, res1, prod0, known, *columns],
        [array(own)],
    )
    return x2.reshape(-1), res2.reshape(-1)


def solution(mesh):
    placed = (
        P(None, ("sector", "rd")),
        P(None, ("sector", "pr")),
        P(("sector", "rd", "pr")),
        P(("sector", "pr", "rd")),
        P(("sector", "pr", "rd")),
        P(("sector", "rd"), "pr", None, None),
        P(("sector", "rd"), "pr"),
    )
    return jax.shard_map(
        functools.partial(body, mesh.shape["rd"], mesh.shape["pr"]),
        mesh=mesh,
        in_specs=placed,
        out_specs=(P(("sector", "pr", "rd")), P(("sector", "pr", "rd"))),
        check_vma=False,
    )
```

profile of v0, /device:TPU:0, one launch (start us, length us, event | category | flops | bytes accessed | tf_op | source)
XLA Modules:
  0.0 66.4 jit_solution(4247519205875974596)
XLA Ops:
  4.5 2.4 %collective-permute-start.2 = (f32[65,4,128]{2,1,0:T(4,128)S(1)}, f32[65,4,128]{2,1,0:T(4,128)S(1)}, u32[]{:S(2)}, u32[]{:S(2)}) collective-permute-start(f32[65,4,128]{2,1,0:T(4,128)S(1)} %get-tuple-element.25.refs_5_), channel_id=1, source_target_pairs={{0,12},{4,8},{8,4},{12,0},{1,13},{5,9},{9,5},{13,1},{2,14},{6,10},... | collective-permute-start | bytes 399368 | tf_op jit(solution)/shard_map/ppermute | solution.py:408
  7.7 1.2 %copy-done.2 = f32[3,65536]{1,0:T(4,128)S(1)} copy-done((f32[3,65536]{1,0:T(4,128)S(1)}, f32[3,65536]{1,0:T(4,128)}, u32[]{:S(2)}) %copy-start.2) | copy-done | bytes 786456
  9.8 2.9 %tiles.1.refs_4_.refs_2_.refs_3_ = f32[1280,8,512]{2,1,0:T(8,128)S(1)} custom-call(s32[2,20]{1,0:T(2,128)S(4)} %get-tuple-element.23.table.refs_0_, s32[8]{0:T(128)S(4)} %get-tuple-element.24.ids.refs_1_, s32[3]{0:T(128)S(4)} %get-tuple-element.22.info.refs_2_.refs_1_.refs_0_, f32[3,16384]{1,0:T(4,128)S(1)} %copy-done.5, f32[3,65536]{1,0:T(4,128)S(1)} %copy-done.2), custom_call_target="tpu_custom_call" | custom-call | tf_op jit(solution)/shard_map/tiles/pallas_call | solution.py:28
  12.7 1.2 %collective-permute-done.1.refs_7_ = f32[65,4,128]{2,1,0:T(4,128)S(1)} collective-permute-done((f32[65,4,128]{2,1,0:T(4,128)S(1)}, f32[65,4,128]{2,1,0:T(4,128)S(1)}, u32[]{:S(2)}, u32[]{:S(2)}) %collective-permute-start.1) | collective-permute-done | bytes 133152 | tf_op jit(solution)/shard_map/ppermute | solution.py:408
  13.9 1.1 %first_forward.1 = (f32[32,4,128]{2,1,0:T(4,128)S(1)}, f32[8,4,128]{2,1,0:T(4,128)S(1)}, f32[8,4,128]{2,1,0:T(4,128)S(1)}, s32[4,4,128]{2,1,0:T(4,128)S(4)}) custom-call(s32[2,20]{1,0:T(2,128)S(4)} %get-tuple-element.23.table.refs_0_, s32[8]{0:T(128)S(4)} %get-tuple-element.24.ids.refs_1_, s32[3]{0:T(128)S(4)} %get-tuple-element.22.info.refs_2_.refs_1_.refs_0_, ...), custom_call_target="tpu_custom_call" | custom-call | tf_op jit(solution)/shard_map/first_forward/pallas_call | solution.py:28
  15.0 6.9 %collective-permute-start.5 = (f32[32,4,128]{2,1,0:T(4,128)S(1)}, f32[32,4,128]{2,1,0:T(4,128)S(1)}, u32[]{:S(2)}, u32[]{:S(2)}) collective-permute-start(f32[32,4,128]{2,1,0:T(4,128)S(1)} %get-tuple-element.29.refs_3_), channel_id=1, source_target_pairs={{0,3},{1,2},{2,1},{3,0},{4,7},{5,6},{6,5},{7,4},{8,11},{9,10},{10,... | collective-permute-start | bytes 196616 | tf_op jit(solution)/shard_map/ppermute | solution.py:408
  22.6 1.8 %collective-permute-done.5.refs_6_ = f32[32,4,128]{2,1,0:T(4,128)S(1)} collective-permute-done((f32[32,4,128]{2,1,0:T(4,128)S(1)}, f32[32,4,128]{2,1,0:T(4,128)S(1)}, u32[]{:S(2)}, u32[]{:S(2)}) %collective-permute-start.5) | collective-permute-done | bytes 65568 | tf_op jit(solution)/shard_map/ppermute | solution.py:408
  24.4 2.7 %collective-permute-done.4.refs_5_ = f32[32,4,128]{2,1,0:T(4,128)S(1)} collective-permute-done((f32[32,4,128]{2,1,0:T(4,128)S(1)}, f32[32,4,128]{2,1,0:T(4,128)S(1)}, u32[]{:S(2)}, u32[]{:S(2)}) %collective-permute-start.4) | collective-permute-done | bytes 65568 | tf_op jit(solution)/shard_map/ppermute | solution.py:408
  27.1 1.0 %row_0.1.refs_8_ = f32[9,4,128]{2,1,0:T(4,128)S(1)} custom-call(s32[2,20]{1,0:T(2,128)S(4)} %get-tuple-element.23.table.refs_0_, s32[3]{0:T(128)S(4)} %get-tuple-element.22.info.refs_2_.refs_1_.refs_0_, f32[1280,8,512]{2,1,0:T(8,128)S(1)} %tiles.1.refs_4_.refs_2_.refs_3_, f32[32,4,128]{2,1,0:T(4,128)S(1)} %get-tuple-element.29.refs_3_, ...), custom_call_target="tpu_custom_call" | custom-call | tf_op jit(solution)/shard_map/row_0/pallas_call | solution.py:28
  28.9 3.2 %collective-permute-start.7 = (f32[9,4,128]{2,1,0:T(4,128)S(1)}, f32[9,4,128]{2,1,0:T(4,128)S(1)}, u32[]{:S(2)}, u32[]{:S(2)}) collective-permute-start(f32[9,4,128]{2,1,0:T(4,128)S(1)} %row_0.1.refs_8_), channel_id=1, source_target_pairs={{0,8},{4,12},{8,0},{12,4},{1,9},{5,13},{9,1},{13,5},{2,10},{6,14},... | collective-permute-start | bytes 55304 | tf_op jit(solution)/shard_map/ppermute | solution.py:408
  32.1 1.8 %collective-permute-done.7.refs_10_ = f32[9,4,128]{2,1,0:T(4,128)S(1)} collective-permute-done((f32[9,4,128]{2,1,0:T(4,128)S(1)}, f32[9,4,128]{2,1,0:T(4,128)S(1)}, u32[]{:S(2)}, u32[]{:S(2)}) %collective-permute-start.7) | collective-permute-done | bytes 18464 | tf_op jit(solution)/shard_map/ppermute | solution.py:408
  34.7 4.0 %collective-permute-start.11 = (f32[33,4,128]{2,1,0:T(4,128)S(1)}, f32[33,4,128]{2,1,0:T(4,128)S(1)}, u32[]{:S(2)}, u32[]{:S(2)}) collective-permute-start(f32[33,4,128]{2,1,0:T(4,128)S(1)} %get-tuple-element.32.refs_3_), channel_id=1, source_target_pairs={{0,3},{1,2},{2,1},{3,0},{4,7},{5,6},{6,5},{7,4},{8,11},{9,10},{10,... | collective-permute-start | bytes 202760 | tf_op jit(solution)/shard_map/ppermute | solution.py:408
  39.3 2.4 %collective-permute-done.11.refs_6_ = f32[33,4,128]{2,1,0:T(4,128)S(1)} collective-permute-done((f32[33,4,128]{2,1,0:T(4,128)S(1)}, f32[33,4,128]{2,1,0:T(4,128)S(1)}, u32[]{:S(2)}, u32[]{:S(2)}) %collective-permute-start.11) | collective-permute-done | bytes 67616 | tf_op jit(solution)/shard_map/ppermute | solution.py:408
  41.8 2.6 %collective-permute-done.10.refs_5_ = f32[33,4,128]{2,1,0:T(4,128)S(1)} collective-permute-done((f32[33,4,128]{2,1,0:T(4,128)S(1)}, f32[33,4,128]{2,1,0:T(4,128)S(1)}, u32[]{:S(2)}, u32[]{:S(2)}) %collective-permute-start.10) | collective-permute-done | bytes 67616 | tf_op jit(solution)/shard_map/ppermute | solution.py:408
  44.4 1.0 %row_1.1 = (f32[9,4,128]{2,1,0:T(4,128)S(1)}, f32[32,4,128]{2,1,0:T(4,128)S(1)}) custom-call(s32[2,20]{1,0:T(2,128)S(4)} %get-tuple-element.23.table.refs_0_, s32[3]{0:T(128)S(4)} %get-tuple-element.22.info.refs_2_.refs_1_.refs_0_, f32[1280,8,512]{2,1,0:T(8,128)S(1)} %tiles.1.refs_4_.refs_2_.refs_3_, f32[33,4,128]{2,1,0:T(4,128)S(1)} %get-tuple-element.32.refs_3_, ...), custom_call_target="tpu_custom_call" | custom-call | tf_op jit(solution)/shard_map/row_1/pallas_call | solution.py:28
  45.5 1.9 %collective-permute-start.13 = (f32[9,4,128]{2,1,0:T(4,128)S(1)}, f32[9,4,128]{2,1,0:T(4,128)S(1)}, u32[]{:S(2)}, u32[]{:S(2)}) collective-permute-start(f32[9,4,128]{2,1,0:T(4,128)S(1)} %get-tuple-element.33.refs_9_), channel_id=1, source_target_pairs={{0,8},{4,12},{8,0},{12,4},{1,9},{5,13},{9,1},{13,5},{2,10},{6,14},... | collective-permute-start | bytes 55304 | tf_op jit(solution)/shard_map/ppermute | solution.py:408
  47.5 1.2 %collective-permute-done.14.refs_12_ = f32[9,4,128]{2,1,0:T(4,128)S(1)} collective-permute-done((f32[9,4,128]{2,1,0:T(4,128)S(1)}, f32[9,4,128]{2,1,0:T(4,128)S(1)}, u32[]{:S(2)}, u32[]{:S(2)}) %collective-permute-start.14) | collective-permute-done | bytes 18464 | tf_op jit(solution)/shard_map/ppermute | solution.py:408
  50.1 4.4 %collective-permute-start.17 = (f32[33,4,128]{2,1,0:T(4,128)S(1)}, f32[33,4,128]{2,1,0:T(4,128)S(1)}, u32[]{:S(2)}, u32[]{:S(2)}) collective-permute-start(f32[33,4,128]{2,1,0:T(4,128)S(1)} %get-tuple-element.38.refs_3_), channel_id=1, source_target_pairs={{0,3},{1,2},{2,1},{3,0},{4,7},{5,6},{6,5},{7,4},{8,11},{9,10},{10,... | collective-permute-start | bytes 202760 | tf_op jit(solution)/shard_map/ppermute | solution.py:408
  55.2 2.2 %collective-permute-done.17.refs_6_ = f32[33,4,128]{2,1,0:T(4,128)S(1)} collective-permute-done((f32[33,4,128]{2,1,0:T(4,128)S(1)}, f32[33,4,128]{2,1,0:T(4,128)S(1)}, u32[]{:S(2)}, u32[]{:S(2)}) %collective-permute-start.17) | collective-permute-done | bytes 67616 | tf_op jit(solution)/shard_map/ppermute | solution.py:408
  57.3 3.1 %collective-permute-done.16.refs_5_ = f32[33,4,128]{2,1,0:T(4,128)S(1)} collective-permute-done((f32[33,4,128]{2,1,0:T(4,128)S(1)}, f32[33,4,128]{2,1,0:T(4,128)S(1)}, u32[]{:S(2)}, u32[]{:S(2)}) %collective-permute-start.16) | collective-permute-done | bytes 67616 | tf_op jit(solution)/shard_map/ppermute | solution.py:408
  60.4 1.0 %row_2.1.refs_8_ = f32[9,4,128]{2,1,0:T(4,128)S(1)} custom-call(s32[2,20]{1,0:T(2,128)S(4)} %get-tuple-element.23.table.refs_0_, s32[3]{0:T(128)S(4)} %get-tuple-element.22.info.refs_2_.refs_1_.refs_0_, f32[1280,8,512]{2,1,0:T(8,128)S(1)} %tiles.1.refs_4_.refs_2_.refs_3_, f32[33,4,128]{2,1,0:T(4,128)S(1)} %get-tuple-element.38.refs_3_, ...), custom_call_target="tpu_custom_call" | custom-call | tf_op jit(solution)/shard_map/row_2/pallas_call | solution.py:28
  61.5 1.5 %collective-permute-start.19 = (f32[9,4,128]{2,1,0:T(4,128)S(1)}, f32[9,4,128]{2,1,0:T(4,128)S(1)}, u32[]{:S(2)}, u32[]{:S(2)}) collective-permute-start(f32[9,4,128]{2,1,0:T(4,128)S(1)} %row_2.1.refs_8_), channel_id=1, source_target_pairs={{0,8},{4,12},{8,0},{12,4},{1,9},{5,13},{9,1},{13,5},{2,10},{6,14},... | collective-permute-start | bytes 55304 | tf_op jit(solution)/shard_map/ppermute | solution.py:408
  63.3 1.5 %collective-permute-done.20.refs_11_ = f32[9,4,128]{2,1,0:T(4,128)S(1)} collective-permute-done((f32[9,4,128]{2,1,0:T(4,128)S(1)}, f32[9,4,128]{2,1,0:T(4,128)S(1)}, u32[]{:S(2)}, u32[]{:S(2)}) %collective-permute-start.20) | collective-permute-done | bytes 18464 | tf_op jit(solution)/shard_map/ppermute | solution.py:408
  65.3 1.1 %last.1 = (f32[32,4,128]{2,1,0:T(4,128)}, f32[32,4,128]{2,1,0:T(4,128)}) custom-call(s32[3]{0:T(128)S(4)} %get-tuple-element.22.info.refs_2_.refs_1_.refs_0_, s32[4,4,128]{2,1,0:T(4,128)S(4)} %get-tuple-element.26.refs_2_.refs_1_, f32[32,4,128]{2,1,0:T(4,128)S(1)} %bitcast.13, f32[32,4,128]{2,1,0:T(4,128)S(1)} %get-tuple-element.34.refs_3_, ...), custom_call_target="tpu_custom_call" | custom-call | tf_op jit(solution)/shard_map/last/pallas_call | solution.py:28
  (44 shorter events, 10.8 us)
Async XLA Ops:
  0.6 13.3 %copy-start.6 = (f32[4096]{0:T(1024)S(1)}, f32[4096]{0:T(1024)}, u32[]{:S(2)}) copy-start(f32[4096]{0:T(1024)} %param.9) | copy-start | bytes 49156
  4.5 8.2 %collective-permute-start.2 = (f32[65,4,128]{2,1,0:T(4,128)S(1)}, f32[65,4,128]{2,1,0:T(4,128)S(1)}, u32[]{:S(2)}, u32[]{:S(2)}) collective-permute-start(f32[65,4,128]{2,1,0:T(4,128)S(1)} %get-tuple-element.25.refs_5_), channel_id=1, source_target_pairs={{0,12},{4,8},{8,4},{12,0},{1,13},{5,9},{9,5},{13,1},{2,14},{6,10},... | collective-permute-start | bytes 399368 | tf_op jit(solution)/shard_map/ppermute | solution.py:408
  7.0 7.0 %collective-permute-start.1 = (f32[65,4,128]{2,1,0:T(4,128)S(1)}, f32[65,4,128]{2,1,0:T(4,128)S(1)}, u32[]{:S(2)}, u32[]{:S(2)}) collective-permute-start(f32[65,4,128]{2,1,0:T(4,128)S(1)} %get-tuple-element.25.refs_5_), channel_id=1, source_target_pairs={{0,8},{4,12},{8,0},{12,4},{1,9},{5,13},{9,1},{13,5},{2,10},{6,14},... | collective-permute-start | bytes 399368 | tf_op jit(solution)/shard_map/ppermute | solution.py:408
  7.6 6.3 %collective-permute-start = (f32[65,4,128]{2,1,0:T(4,128)S(1)}, f32[65,4,128]{2,1,0:T(4,128)S(1)}, u32[]{:S(2)}, u32[]{:S(2)}) collective-permute-start(f32[65,4,128]{2,1,0:T(4,128)S(1)} %get-tuple-element.25.refs_5_), channel_id=1, source_target_pairs={{0,4},{4,0},{8,12},{12,8},{1,5},{5,1},{9,13},{13,9},{2,6},{6,2},{1... | collective-permute-start | bytes 399368 | tf_op jit(solution)/shard_map/ppermute | solution.py:408
  13.9 20.0 %copy-start.1 = (f32[16384]{0:T(1024)S(1)}, f32[16384]{0:T(1024)}, u32[]{:S(2)}) copy-start(f32[16384]{0:T(1024)} %param.11) | copy-start | bytes 196612
  13.9 20.0 %copy-start.4 = (f32[16384]{0:T(1024)S(1)}, f32[16384]{0:T(1024)}, u32[]{:S(2)}) copy-start(f32[16384]{0:T(1024)} %param.10) | copy-start | bytes 196612
  15.0 9.4 %collective-permute-start.5 = (f32[32,4,128]{2,1,0:T(4,128)S(1)}, f32[32,4,128]{2,1,0:T(4,128)S(1)}, u32[]{:S(2)}, u32[]{:S(2)}) collective-permute-start(f32[32,4,128]{2,1,0:T(4,128)S(1)} %get-tuple-element.29.refs_3_), channel_id=1, source_target_pairs={{0,3},{1,2},{2,1},{3,0},{4,7},{5,6},{6,5},{7,4},{8,11},{9,10},{10,... | collective-permute-start | bytes 196616 | tf_op jit(solution)/shard_map/ppermute | solution.py:408
  22.0 5.2 %collective-permute-start.4 = (f32[32,4,128]{2,1,0:T(4,128)S(1)}, f32[32,4,128]{2,1,0:T(4,128)S(1)}, u32[]{:S(2)}, u32[]{:S(2)}) collective-permute-start(f32[32,4,128]{2,1,0:T(4,128)S(1)} %get-tuple-element.29.refs_3_), channel_id=1, source_target_pairs={{0,2},{1,3},{2,0},{3,1},{4,6},{5,7},{6,4},{7,5},{8,10},{9,11},{10,... | collective-permute-start | bytes 196616 | tf_op jit(solution)/shard_map/ppermute | solution.py:408
  22.0 5.2 %collective-permute-start.3 = (f32[32,4,128]{2,1,0:T(4,128)S(1)}, f32[32,4,128]{2,1,0:T(4,128)S(1)}, u32[]{:S(2)}, u32[]{:S(2)}) collective-permute-start(f32[32,4,128]{2,1,0:T(4,128)S(1)} %get-tuple-element.29.refs_3_), channel_id=1, source_target_pairs={{0,1},{1,0},{2,3},{3,2},{4,5},{5,4},{6,7},{7,6},{8,9},{9,8},{10,11... | collective-permute-start | bytes 196616 | tf_op jit(solution)/shard_map/ppermute | solution.py:408
  28.1 4.0 %collective-permute-start.8 = (f32[9,4,128]{2,1,0:T(4,128)S(1)}, f32[9,4,128]{2,1,0:T(4,128)S(1)}, u32[]{:S(2)}, u32[]{:S(2)}) collective-permute-start(f32[9,4,128]{2,1,0:T(4,128)S(1)} %row_0.1.refs_8_), channel_id=1, source_target_pairs={{0,12},{4,8},{8,4},{12,0},{1,13},{5,9},{9,5},{13,1},{2,14},{6,10},... | collective-permute-start | bytes 55304 | tf_op jit(solution)/shard_map/ppermute | solution.py:408
  28.9 5.0 %collective-permute-start.7 = (f32[9,4,128]{2,1,0:T(4,128)S(1)}, f32[9,4,128]{2,1,0:T(4,128)S(1)}, u32[]{:S(2)}, u32[]{:S(2)}) collective-permute-start(f32[9,4,128]{2,1,0:T(4,128)S(1)} %row_0.1.refs_8_), channel_id=1, source_target_pairs={{0,8},{4,12},{8,0},{12,4},{1,9},{5,13},{9,1},{13,5},{2,10},{6,14},... | collective-permute-start | bytes 55304 | tf_op jit(solution)/shard_map/ppermute | solution.py:408
  32.1 1.9 %collective-permute-start.6 = (f32[9,4,128]{2,1,0:T(4,128)S(1)}, f32[9,4,128]{2,1,0:T(4,128)S(1)}, u32[]{:S(2)}, u32[]{:S(2)}) collective-permute-start(f32[9,4,128]{2,1,0:T(4,128)S(1)} %row_0.1.refs_8_), channel_id=1, source_target_pairs={{0,4},{4,0},{8,12},{12,8},{1,5},{5,1},{9,13},{13,9},{2,6},{6,2},{1... | collective-permute-start | bytes 55304 | tf_op jit(solution)/shard_map/ppermute | solution.py:408
  34.7 7.1 %collective-permute-start.11 = (f32[33,4,128]{2,1,0:T(4,128)S(1)}, f32[33,4,128]{2,1,0:T(4,128)S(1)}, u32[]{:S(2)}, u32[]{:S(2)}) collective-permute-start(f32[33,4,128]{2,1,0:T(4,128)S(1)} %get-tuple-element.32.refs_3_), channel_id=1, source_target_pairs={{0,3},{1,2},{2,1},{3,0},{4,7},{5,6},{6,5},{7,4},{8,11},{9,10},{10,... | collective-permute-start | bytes 202760 | tf_op jit(solution)/shard_map/ppermute | solution.py:408
  38.7 5.7 %collective-permute-start.10 = (f32[33,4,128]{2,1,0:T(4,128)S(1)}, f32[33,4,128]{2,1,0:T(4,128)S(1)}, u32[]{:S(2)}, u32[]{:S(2)}) collective-permute-start(f32[33,4,128]{2,1,0:T(4,128)S(1)} %get-tuple-element.32.refs_3_), channel_id=1, source_target_pairs={{0,2},{1,3},{2,0},{3,1},{4,6},{5,7},{6,4},{7,5},{8,10},{9,11},{10,... | collective-permute-start | bytes 202760 | tf_op jit(solution)/shard_map/ppermute | solution.py:408
  38.7 5.7 %collective-permute-start.9 = (f32[33,4,128]{2,1,0:T(4,128)S(1)}, f32[33,4,128]{2,1,0:T(4,128)S(1)}, u32[]{:S(2)}, u32[]{:S(2)}) collective-permute-start(f32[33,4,128]{2,1,0:T(4,128)S(1)} %get-tuple-element.32.refs_3_), channel_id=1, source_target_pairs={{0,1},{1,0},{2,3},{3,2},{4,5},{5,4},{6,7},{7,6},{8,9},{9,8},{10,11... | collective-permute-start | bytes 202760 | tf_op jit(solution)/shard_map/ppermute | solution.py:408
  45.4 3.2 %collective-permute-start.14 = (f32[9,4,128]{2,1,0:T(4,128)S(1)}, f32[9,4,128]{2,1,0:T(4,128)S(1)}, u32[]{:S(2)}, u32[]{:S(2)}) collective-permute-start(f32[9,4,128]{2,1,0:T(4,128)S(1)} %get-tuple-element.33.refs_9_), channel_id=1, source_target_pairs={{0,12},{4,8},{8,4},{12,0},{1,13},{5,9},{9,5},{13,1},{2,14},{6,10},... | collective-permute-start | bytes 55304 | tf_op jit(solution)/shard_map/ppermute | solution.py:408
  45.5 3.8 %collective-permute-start.13 = (f32[9,4,128]{2,1,0:T(4,128)S(1)}, f32[9,4,128]{2,1,0:T(4,128)S(1)}, u32[]{:S(2)}, u32[]{:S(2)}) collective-permute-start(f32[9,4,128]{2,1,0:T(4,128)S(1)} %get-tuple-element.33.refs_9_), channel_id=1, source_target_pairs={{0,8},{4,12},{8,0},{12,4},{1,9},{5,13},{9,1},{13,5},{2,10},{6,14},... | collective-permute-start | bytes 55304 | tf_op jit(solution)/shard_map/ppermute | solution.py:408
  47.4 1.9 %collective-permute-start.12 = (f32[9,4,128]{2,1,0:T(4,128)S(1)}, f32[9,4,128]{2,1,0:T(4,128)S(1)}, u32[]{:S(2)}, u32[]{:S(2)}) collective-permute-start(f32[9,4,128]{2,1,0:T(4,128)S(1)} %get-tuple-element.33.refs_9_), channel_id=1, source_target_pairs={{0,4},{4,0},{8,12},{12,8},{1,5},{5,1},{9,13},{13,9},{2,6},{6,2},{1... | collective-permute-start | bytes 55304 | tf_op jit(solution)/shard_map/ppermute | solution.py:408
  50.1 7.2 %collective-permute-start.17 = (f32[33,4,128]{2,1,0:T(4,128)S(1)}, f32[33,4,128]{2,1,0:T(4,128)S(1)}, u32[]{:S(2)}, u32[]{:S(2)}) collective-permute-start(f32[33,4,128]{2,1,0:T(4,128)S(1)} %get-tuple-element.38.refs_3_), channel_id=1, source_target_pairs={{0,3},{1,2},{2,1},{3,0},{4,7},{5,6},{6,5},{7,4},{8,11},{9,10},{10,... | collective-permute-start | bytes 202760 | tf_op jit(solution)/shard_map/ppermute | solution.py:408
  54.5 5.9 %collective-permute-start.16 = (f32[33,4,128]{2,1,0:T(4,128)S(1)}, f32[33,4,128]{2,1,0:T(4,128)S(1)}, u32[]{:S(2)}, u32[]{:S(2)}) collective-permute-start(f32[33,4,128]{2,1,0:T(4,128)S(1)} %get-tuple-element.38.refs_3_), channel_id=1, source_target_pairs={{0,2},{1,3},{2,0},{3,1},{4,6},{5,7},{6,4},{7,5},{8,10},{9,11},{10,... | collective-permute-start | bytes 202760 | tf_op jit(solution)/shard_map/ppermute | solution.py:408
  54.5 5.9 %collective-permute-start.15 = (f32[33,4,128]{2,1,0:T(4,128)S(1)}, f32[33,4,128]{2,1,0:T(4,128)S(1)}, u32[]{:S(2)}, u32[]{:S(2)}) collective-permute-start(f32[33,4,128]{2,1,0:T(4,128)S(1)} %get-tuple-element.38.refs_3_), channel_id=1, source_target_pairs={{0,1},{1,0},{2,3},{3,2},{4,5},{5,4},{6,7},{7,6},{8,9},{9,8},{10,11... | collective-permute-start | bytes 202760 | tf_op jit(solution)/shard_map/ppermute | solution.py:408
  61.4 3.4 %collective-permute-start.20 = (f32[9,4,128]{2,1,0:T(4,128)S(1)}, f32[9,4,128]{2,1,0:T(4,128)S(1)}, u32[]{:S(2)}, u32[]{:S(2)}) collective-permute-start(f32[9,4,128]{2,1,0:T(4,128)S(1)} %row_2.1.refs_8_), channel_id=1, source_target_pairs={{0,12},{4,8},{8,4},{12,0},{1,13},{5,9},{9,5},{13,1},{2,14},{6,10},... | collective-permute-start | bytes 55304 | tf_op jit(solution)/shard_map/ppermute | solution.py:408
  61.5 3.8 %collective-permute-start.19 = (f32[9,4,128]{2,1,0:T(4,128)S(1)}, f32[9,4,128]{2,1,0:T(4,128)S(1)}, u32[]{:S(2)}, u32[]{:S(2)}) collective-permute-start(f32[9,4,128]{2,1,0:T(4,128)S(1)} %row_2.1.refs_8_), channel_id=1, source_target_pairs={{0,8},{4,12},{8,0},{12,4},{1,9},{5,13},{9,1},{13,5},{2,10},{6,14},... | collective-permute-start | bytes 55304 | tf_op jit(solution)/shard_map/ppermute | solution.py:408
  63.0 2.3 %collective-permute-start.18 = (f32[9,4,128]{2,1,0:T(4,128)S(1)}, f32[9,4,128]{2,1,0:T(4,128)S(1)}, u32[]{:S(2)}, u32[]{:S(2)}) collective-permute-start(f32[9,4,128]{2,1,0:T(4,128)S(1)} %row_2.1.refs_8_), channel_id=1, source_target_pairs={{0,4},{4,0},{8,12},{12,8},{1,5},{5,1},{9,13},{13,9},{2,6},{6,2},{1... | collective-permute-start | bytes 55304 | tf_op jit(solution)/shard_map/ppermute | solution.py:408
  (5 other events, 4.5 us)
where the time goes:
time: 67.2 us; the launch traced here: 66.4 us
  starting transfers between devices  28.3 us (42%)
  waiting for transfers between devices  21.7 us (32%)
  Pallas kernels  10.3 us (15%)
  local copies, waits for them, and re-layouts  4.54 us (7%)
  between operations  1.4 us (2%)
    ppermute x21, starting transfers between devices, exchange(): got.append(lax.ppermute(values, axis, pairs))  28.3 us
    ppermute x21, waiting for transfers between devices, exchange(): got.append(lax.ppermute(values, axis, pairs))  21.7 us
    pallas_call x9, Pallas kernels, call(): pl.pallas_call(kernel, name=name, out_shape=outs, in_specs=[pl.BlockSpec(...  10.3 us
    unnamed x16, local copies, waits for them, and re-layouts  4.54 us
  transfers between devices with their start and end apart: 21, of which 12 were waited for; matrix products, arithmetic and copies ran while one was open for 0% of the time, Pallas kernels for 4%

commit v1 on v0

--- a/solution.py
+++ b/solution.py
@@ -22,6 +22,7 @@
 I32 = jnp.int32
 VMEM = pltpu.VMEM
 SMEM = pltpu.SMEM
+HBM = pltpu.HBM
 
 
 def call(kernel, name, room, outs, ins, args, scratch=()):
@@ -40,8 +41,13 @@
     return lax.broadcasted_iota(jnp.int32, shape, len(shape) - 1)
 
 
-def each(count, one):
-    lax.fori_loop(0, count, lambda i, carry: (one(i), carry)[1], 0)
+def each(count, spare, one):
+    def two(i, carry):
+        one(2 * i)
+        one(jnp.where(2 * i + 1 < count, 2 * i + 1, spare))
+        return carry
+
+    lax.fori_loop(0, (count + 1) // 2, two, 0)
 
 
 def over(n, one, carry=0):
@@ -62,19 +68,21 @@
     return jnp.sum(jnp.sum(values, axis=0), keepdims=True)
 
 
-def prep_kernel(pairs, count, place, x0, damp, payload, table, ids, info, sems):
+def prep_kernel(pairs_in, count, place, x0, damp, payload, table, ids, info, pairs, sems):
     own = x0.shape[0]
     slots = ids.shape[0]
     copies = [
         pltpu.make_async_copy(x0, payload.at[pl.ds(0, own)], sems.at[0]),
         pltpu.make_async_copy(damp, payload.at[pl.ds(own, own)], sems.at[1]),
     ]
-    for copy in copies:
+    pairs_copy = pltpu.make_async_copy(pairs_in, pairs, sems.at[2])
+    for copy in [pairs_copy, *copies]:
         copy.start()
     for s in range(slots):
         ids[s] = -1
     info[0] = place[0]
     info[1] = place[1]
+    pairs_copy.wait()
     info[2] = count[0, 0]
 
     def assign(i, carry):
@@ -89,6 +97,8 @@
         return carry
 
     lax.fori_loop(0, count[0, 0], assign, 0)
+    table[0, pairs.shape[1]] = 0
+    table[1, pairs.shape[1]] = 0
     payload[2 * own] = scalar_tile([ids[s].astype(F32) for s in range(slots)])
     for copy in copies:
         copy.wait()
@@ -175,6 +185,11 @@
 
     lax.fori_loop(0, (count + 1) // 2, two, 0)
 
+    @pl.when(count % 2 == 1)
+    def _():
+        spare = tiles.at[pl.ds(tiles.shape[0] - GROUPS, GROUPS)]
+        spare[...] = jnp.zeros(spare.shape, F32)
+
 
 def spread_lanes(need, spread):
     slots = need.shape[0]
@@ -211,7 +226,7 @@
         added = [jnp.sum(sums[0][c] + sums[1][c], axis=0, keepdims=True) for c in range(ROWS)]
         out[a] += jnp.concatenate(added, axis=0)
 
-    each(count, one)
+    each(count, table.shape[1] - 1, one)
 
 
 def adjoint_tiles(table, count, tiles, row, wide, out):
@@ -228,7 +243,7 @@
             t = [tile[v, :, c * LANES : (c + 1) * LANES] * spread[c] for c in range(ROWS)]
             held[v] += (t[0] + t[1]) + (t[2] + t[3])
 
-    each(count, one)
+    each(count, table.shape[1] - 1, one)
     lane = lane_index((8, LANES))
 
     def reduce(s, groups):
@@ -420,6 +435,7 @@
     place = jnp.stack([lax.axis_index("rd"), lax.axis_index("pr")]).astype(I32)
     array = lambda *lead: VMEM((*lead, ROWS, LANES), F32)
     wide = VMEM((slots * GROUPS, 8, LANES), F32)
+    far = lambda v: pltpu.with_memory_space_constraint(v, HBM)
     dma = pltpu.SemaphoreType.DMA
     room = 5 + slots * GROUPS * 8 * LANES * 4 // MIB
 
@@ -427,19 +443,19 @@
         prep_kernel,
         "prep",
         room,
-        [array(2 * own + 1), SMEM((2, cap), I32), SMEM((slots,), I32), SMEM((3,), I32)],
-        [SMEM, SMEM, SMEM, pl.ANY, pl.ANY],
-        [pairs, pair_count, place, x0, damp],
-        [dma((2,))],
+        [array(2 * own + 1), SMEM((2, cap + 1), I32), SMEM((slots,), I32), SMEM((3,), I32)],
+        [HBM, SMEM, SMEM, HBM, HBM],
+        [far(pairs), pair_count, place, far(x0), far(damp)],
+        [SMEM((2, cap), I32), dma((3,))],
     )
     columns = exchange(payload, "rd", n_rd)
     (tiles,) = call(
         tiles_kernel,
         "tiles",
         room + slots * FEATURES * BLK * 4 // MIB,
-        [VMEM((cap * GROUPS, 8, BLK), F32)],
-        [SMEM, SMEM, SMEM, pl.ANY, pl.ANY],
-        [table, ids, info, reading_geo, prism_geo],
+        [VMEM(((cap + 1) * GROUPS, 8, BLK), F32)],
+        [SMEM, SMEM, SMEM, HBM, HBM],
+        [table, ids, info, far(reading_geo), far(prism_geo)],
         [
             VMEM((cap, 8, BLK), F32),
             VMEM((slots, 8, BLK), F32),

time: 67.2 us -> 63.9 us (0.951); the launches traced: 66.4 us -> 64.3 us
  Pallas kernels: 10.3 us -> 21.5 us
  starting transfers between devices: 28.3 us -> 22.6 us
  local copies, waits for them, and re-layouts: 4.54 us -> 0.02 us
  waiting for transfers between devices: 21.7 us -> 18.7 us
    pallas_call x9, Pallas kernels: 10.3 us -> 21.5 us  [call(): pl.pallas_call(kernel, name=name, out_shape=outs, in_specs=[pl.BlockSpec(...]
    ppermute x21, starting transfers between devices: 28.3 us -> 22.6 us  [exchange(): got.append(lax.ppermute(values, axis, pairs))]
    unnamed x16 -> x6, local copies, waits for them, and re-layouts: 4.54 us -> 0.02 us
    ppermute x21, waiting for transfers between devices: 21.7 us -> 18.7 us  [exchange(): got.append(lax.ppermute(values, axis, pairs))]
  transfers between devices with their start and end apart: 21 -> 21, of which waited for: 12 -> 13; matrix products, arithmetic and copies ran while one was open for 0% -> 0% of each run, Pallas kernels for 4% -> 11%
where the time goes in v1:
time: 63.9 us; the launch traced here: 64.3 us
  starting transfers between devices  22.6 us (35%)
  Pallas kernels  21.5 us (34%)
  waiting for transfers between devices  18.7 us (29%)
  between operations  1.44 us (2%)
    ppermute x21, starting transfers between devices, exchange(): got.append(lax.ppermute(values, axis, pairs))  22.6 us
    pallas_call x9, Pallas kernels, call(): pl.pallas_call(kernel, name=name, out_shape=outs, in_specs=[pl.BlockSpec(...  21.5 us
    ppermute x21, waiting for transfers between devices, exchange(): got.append(lax.ppermute(values, axis, pairs))  18.7 us
  transfers between devices with their start and end apart: 21, of which 13 were waited for; matrix products, arithmetic and copies ran while one was open for 0% of the time, Pallas kernels for 11%

profile of v1, /device:TPU:0, one launch (start us, length us, event | category | flops | bytes accessed | tf_op | source)
XLA Modules:
  0.0 64.3 jit_solution(2411662310433236506)
XLA Ops:
  1.4 1.6 %prep.1 = (f32[65,4,128]{2,1,0:T(4,128)S(1)}, s32[2,21]{1,0:T(2,128)S(4)}, s32[8]{0:T(128)S(4)}, s32[3]{0:T(128)S(4)}) custom-call(s32[2,20]{1,0:T(2,128)} %bitcast.18, s32[1,1]{1,0:T(1,128)S(6)} %copy.9.count, s32[2]{0:T(128)S(1)} %pad_add_fusion.place, f32[32,4,128]{2,1,0:T(4,128)} %bitcast.14, f32[32,4,128]{2,1,0:T(4,128)} %bitcast.10), custom_call_target="tpu_custom_call" | custom-call | tf_op jit(solution)/shard_map/prep/pallas_call | solution.py:29
  2.9 2.3 %collective-permute-start.2 = (f32[65,4,128]{2,1,0:T(4,128)S(1)}, f32[65,4,128]{2,1,0:T(4,128)S(1)}, u32[]{:S(2)}, u32[]{:S(2)}) collective-permute-start(f32[65,4,128]{2,1,0:T(4,128)S(1)} %get-tuple-element.25.refs_5_), channel_id=1, source_target_pairs={{0,12},{4,8},{8,4},{12,0},{1,13},{5,9},{9,5},{13,1},{2,14},{6,10},... | collective-permute-start | bytes 399368 | tf_op jit(solution)/shard_map/ppermute | solution.py:423
  5.9 7.4 %tiles.1.refs_4_.refs_2_.refs_3_ = f32[1344,8,512]{2,1,0:T(8,128)S(1)} custom-call(s32[2,21]{1,0:T(2,128)S(4)} %get-tuple-element.23.table.refs_0_, s32[8]{0:T(128)S(4)} %get-tuple-element.24.ids.refs_1_, s32[3]{0:T(128)S(4)} %get-tuple-element.22.info.refs_2_.refs_1_.refs_0_, f32[3,16384]{1,0:T(4,128)} %readings.1, f32[3,65536]{1,0:T(4,128)} %prisms.1), custom_call_target="tpu_custom_call" | custom-call | tf_op jit(solution)/shard_map/tiles/pallas_call | solution.py:29
  13.4 1.8 %first_forward.1 = (f32[32,4,128]{2,1,0:T(4,128)S(1)}, f32[8,4,128]{2,1,0:T(4,128)S(1)}, f32[8,4,128]{2,1,0:T(4,128)S(1)}, s32[4,4,128]{2,1,0:T(4,128)S(4)}) custom-call(s32[2,21]{1,0:T(2,128)S(4)} %get-tuple-element.23.table.refs_0_, s32[8]{0:T(128)S(4)} %get-tuple-element.24.ids.refs_1_, s32[3]{0:T(128)S(4)} %get-tuple-element.22.info.refs_2_.refs_1_.refs_0_, ...), custom_call_target="tpu_custom_call" | custom-call | tf_op jit(solution)/shard_map/first_forward/pallas_call | solution.py:29
  15.2 2.6 %collective-permute-start.5 = (f32[32,4,128]{2,1,0:T(4,128)S(1)}, f32[32,4,128]{2,1,0:T(4,128)S(1)}, u32[]{:S(2)}, u32[]{:S(2)}) collective-permute-start(f32[32,4,128]{2,1,0:T(4,128)S(1)} %get-tuple-element.29.refs_3_), channel_id=1, source_target_pairs={{0,3},{1,2},{2,1},{3,0},{4,7},{5,6},{6,5},{7,4},{8,11},{9,10},{10,... | collective-permute-start | bytes 196616 | tf_op jit(solution)/shard_map/ppermute | solution.py:423
  17.8 1.9 %collective-permute-start.4 = (f32[32,4,128]{2,1,0:T(4,128)S(1)}, f32[32,4,128]{2,1,0:T(4,128)S(1)}, u32[]{:S(2)}, u32[]{:S(2)}) collective-permute-start(f32[32,4,128]{2,1,0:T(4,128)S(1)} %get-tuple-element.29.refs_3_), channel_id=1, source_target_pairs={{0,2},{1,3},{2,0},{3,1},{4,6},{5,7},{6,4},{7,5},{8,10},{9,11},{10,... | collective-permute-start | bytes 196616 | tf_op jit(solution)/shard_map/ppermute | solution.py:423
  21.4 4.2 %collective-permute-done.4.refs_5_ = f32[32,4,128]{2,1,0:T(4,128)S(1)} collective-permute-done((f32[32,4,128]{2,1,0:T(4,128)S(1)}, f32[32,4,128]{2,1,0:T(4,128)S(1)}, u32[]{:S(2)}, u32[]{:S(2)}) %collective-permute-start.4) | collective-permute-done | bytes 65568 | tf_op jit(solution)/shard_map/ppermute | solution.py:423
  25.6 2.0 %row_0.1.refs_8_ = f32[9,4,128]{2,1,0:T(4,128)S(1)} custom-call(s32[2,21]{1,0:T(2,128)S(4)} %get-tuple-element.23.table.refs_0_, s32[3]{0:T(128)S(4)} %get-tuple-element.22.info.refs_2_.refs_1_.refs_0_, f32[1344,8,512]{2,1,0:T(8,128)S(1)} %tiles.1.refs_4_.refs_2_.refs_3_, f32[32,4,128]{2,1,0:T(4,128)S(1)} %get-tuple-element.29.refs_3_, ...), custom_call_target="tpu_custom_call" | custom-call | tf_op jit(solution)/shard_map/row_0/pallas_call | solution.py:29
  27.9 1.5 %collective-permute-start.6 = (f32[9,4,128]{2,1,0:T(4,128)S(1)}, f32[9,4,128]{2,1,0:T(4,128)S(1)}, u32[]{:S(2)}, u32[]{:S(2)}) collective-permute-start(f32[9,4,128]{2,1,0:T(4,128)S(1)} %row_0.1.refs_8_), channel_id=1, source_target_pairs={{0,4},{4,0},{8,12},{12,8},{1,5},{5,1},{9,13},{13,9},{2,6},{6,2},{1... | collective-permute-start | bytes 55304 | tf_op jit(solution)/shard_map/ppermute | solution.py:423
  29.4 1.3 %collective-permute-done.8.refs_11_ = f32[9,4,128]{2,1,0:T(4,128)S(1)} collective-permute-done((f32[9,4,128]{2,1,0:T(4,128)S(1)}, f32[9,4,128]{2,1,0:T(4,128)S(1)}, u32[]{:S(2)}, u32[]{:S(2)}) %collective-permute-start.8) | collective-permute-done | bytes 18464 | tf_op jit(solution)/shard_map/ppermute | solution.py:423
  31.4 1.8 %second_forward.1 = (f32[33,4,128]{2,1,0:T(4,128)S(1)}, f32[32,4,128]{2,1,0:T(4,128)S(1)}, f32[8,4,128]{2,1,0:T(4,128)S(1)}) custom-call(s32[2,21]{1,0:T(2,128)S(4)} %get-tuple-element.23.table.refs_0_, s32[3]{0:T(128)S(4)} %get-tuple-element.22.info.refs_2_.refs_1_.refs_0_, s32[4,4,128]{2,1,0:T(4,128)S(4)} %get-tuple-element.26.refs_2_.refs_1_, ...), custom_call_target="tpu_custom_call" | custom-call | tf_op jit(solution)/shard_map/second_forward/pallas_call | solution.py:29
  34.5 3.1 %collective-permute-start.9 = (f32[33,4,128]{2,1,0:T(4,128)S(1)}, f32[33,4,128]{2,1,0:T(4,128)S(1)}, u32[]{:S(2)}, u32[]{:S(2)}) collective-permute-start(f32[33,4,128]{2,1,0:T(4,128)S(1)} %get-tuple-element.32.refs_3_), channel_id=1, source_target_pairs={{0,1},{1,0},{2,3},{3,2},{4,5},{5,4},{6,7},{7,6},{8,9},{9,8},{10,11... | collective-permute-start | bytes 202760 | tf_op jit(solution)/shard_map/ppermute | solution.py:423
  37.7 2.5 %collective-permute-done.11.refs_6_ = f32[33,4,128]{2,1,0:T(4,128)S(1)} collective-permute-done((f32[33,4,128]{2,1,0:T(4,128)S(1)}, f32[33,4,128]{2,1,0:T(4,128)S(1)}, u32[]{:S(2)}, u32[]{:S(2)}) %collective-permute-start.11) | collective-permute-done | bytes 67616 | tf_op jit(solution)/shard_map/ppermute | solution.py:423
  41.1 2.0 %row_1.1 = (f32[9,4,128]{2,1,0:T(4,128)S(1)}, f32[32,4,128]{2,1,0:T(4,128)S(1)}) custom-call(s32[2,21]{1,0:T(2,128)S(4)} %get-tuple-element.23.table.refs_0_, s32[3]{0:T(128)S(4)} %get-tuple-element.22.info.refs_2_.refs_1_.refs_0_, f32[1344,8,512]{2,1,0:T(8,128)S(1)} %tiles.1.refs_4_.refs_2_.refs_3_, f32[33,4,128]{2,1,0:T(4,128)S(1)} %get-tuple-element.32.refs_3_, ...), custom_call_target="tpu_custom_call" | custom-call | tf_op jit(solution)/shard_map/row_1/pallas_call | solution.py:29
  43.3 1.7 %collective-permute-start.12 = (f32[9,4,128]{2,1,0:T(4,128)S(1)}, f32[9,4,128]{2,1,0:T(4,128)S(1)}, u32[]{:S(2)}, u32[]{:S(2)}) collective-permute-start(f32[9,4,128]{2,1,0:T(4,128)S(1)} %get-tuple-element.33.refs_9_), channel_id=1, source_target_pairs={{0,4},{4,0},{8,12},{12,8},{1,5},{5,1},{9,13},{13,9},{2,6},{6,2},{1... | collective-permute-start | bytes 55304 | tf_op jit(solution)/shard_map/ppermute | solution.py:423
  45.0 1.3 %collective-permute-done.14.refs_12_ = f32[9,4,128]{2,1,0:T(4,128)S(1)} collective-permute-done((f32[9,4,128]{2,1,0:T(4,128)S(1)}, f32[9,4,128]{2,1,0:T(4,128)S(1)}, u32[]{:S(2)}, u32[]{:S(2)}) %collective-permute-start.14) | collective-permute-done | bytes 18464 | tf_op jit(solution)/shard_map/ppermute | solution.py:423
  47.0 1.9 %third_forward.1 = (f32[33,4,128]{2,1,0:T(4,128)S(1)}, f32[32,4,128]{2,1,0:T(4,128)S(1)}, f32[32,4,128]{2,1,0:T(4,128)S(1)}, f32[32,4,128]{2,1,0:T(4,128)S(1)}, f32[1,4,128]{2,1,0:T(4,128)S(1)}) custom-call(s32[2,21]{1,0:T(2,128)S(4)} %get-tuple-element.23.table.refs_0_, s32[3]{0:T(128)S(4)} %get-tuple-element.22.info.refs_2_.refs_1_.refs_0_, ...), custom_call_target="tpu_custom_call" | custom-call | tf_op jit(solution)/shard_map/third_forward/pallas_call | solution.py:29
  49.0 2.0 %collective-permute-start.16 = (f32[33,4,128]{2,1,0:T(4,128)S(1)}, f32[33,4,128]{2,1,0:T(4,128)S(1)}, u32[]{:S(2)}, u32[]{:S(2)}) collective-permute-start(f32[33,4,128]{2,1,0:T(4,128)S(1)} %get-tuple-element.38.refs_3_), channel_id=1, source_target_pairs={{0,2},{1,3},{2,0},{3,1},{4,6},{5,7},{6,4},{7,5},{8,10},{9,11},{10,... | collective-permute-start | bytes 202760 | tf_op jit(solution)/shard_map/ppermute | solution.py:423
  50.9 2.4 %collective-permute-start.15 = (f32[33,4,128]{2,1,0:T(4,128)S(1)}, f32[33,4,128]{2,1,0:T(4,128)S(1)}, u32[]{:S(2)}, u32[]{:S(2)}) collective-permute-start(f32[33,4,128]{2,1,0:T(4,128)S(1)} %get-tuple-element.38.refs_3_), channel_id=1, source_target_pairs={{0,1},{1,0},{2,3},{3,2},{4,5},{5,4},{6,7},{7,6},{8,9},{9,8},{10,11... | collective-permute-start | bytes 202760 | tf_op jit(solution)/shard_map/ppermute | solution.py:423
  53.3 2.4 %collective-permute-done.17.refs_6_ = f32[33,4,128]{2,1,0:T(4,128)S(1)} collective-permute-done((f32[33,4,128]{2,1,0:T(4,128)S(1)}, f32[33,4,128]{2,1,0:T(4,128)S(1)}, u32[]{:S(2)}, u32[]{:S(2)}) %collective-permute-start.17) | collective-permute-done | bytes 67616 | tf_op jit(solution)/shard_map/ppermute | solution.py:423
  55.8 1.6 %collective-permute-done.16.refs_5_ = f32[33,4,128]{2,1,0:T(4,128)S(1)} collective-permute-done((f32[33,4,128]{2,1,0:T(4,128)S(1)}, f32[33,4,128]{2,1,0:T(4,128)S(1)}, u32[]{:S(2)}, u32[]{:S(2)}) %collective-permute-start.16) | collective-permute-done | bytes 67616 | tf_op jit(solution)/shard_map/ppermute | solution.py:423
  57.4 2.0 %row_2.1.refs_8_ = f32[9,4,128]{2,1,0:T(4,128)S(1)} custom-call(s32[2,21]{1,0:T(2,128)S(4)} %get-tuple-element.23.table.refs_0_, s32[3]{0:T(128)S(4)} %get-tuple-element.22.info.refs_2_.refs_1_.refs_0_, f32[1344,8,512]{2,1,0:T(8,128)S(1)} %tiles.1.refs_4_.refs_2_.refs_3_, f32[33,4,128]{2,1,0:T(4,128)S(1)} %get-tuple-element.38.refs_3_, ...), custom_call_target="tpu_custom_call" | custom-call | tf_op jit(solution)/shard_map/row_2/pallas_call | solution.py:29
  59.9 1.4 %collective-permute-start.18 = (f32[9,4,128]{2,1,0:T(4,128)S(1)}, f32[9,4,128]{2,1,0:T(4,128)S(1)}, u32[]{:S(2)}, u32[]{:S(2)}) collective-permute-start(f32[9,4,128]{2,1,0:T(4,128)S(1)} %row_2.1.refs_8_), channel_id=1, source_target_pairs={{0,4},{4,0},{8,12},{12,8},{1,5},{5,1},{9,13},{13,9},{2,6},{6,2},{1... | collective-permute-start | bytes 55304 | tf_op jit(solution)/shard_map/ppermute | solution.py:423
  61.3 1.3 %collective-permute-done.20.refs_11_ = f32[9,4,128]{2,1,0:T(4,128)S(1)} collective-permute-done((f32[9,4,128]{2,1,0:T(4,128)S(1)}, f32[9,4,128]{2,1,0:T(4,128)S(1)}, u32[]{:S(2)}, u32[]{:S(2)}) %collective-permute-start.20) | collective-permute-done | bytes 18464 | tf_op jit(solution)/shard_map/ppermute | solution.py:423
  (34 shorter events, 8.8 us)
Async XLA Ops:
  0.6 12.7 %copy-start.2 = (f32[4096]{0:T(1024)S(1)}, f32[4096]{0:T(1024)}, u32[]{:S(2)}) copy-start(f32[4096]{0:T(1024)} %param.9) | copy-start | bytes 49156
  2.9 10.4 %collective-permute-start.2 = (f32[65,4,128]{2,1,0:T(4,128)S(1)}, f32[65,4,128]{2,1,0:T(4,128)S(1)}, u32[]{:S(2)}, u32[]{:S(2)}) collective-permute-start(f32[65,4,128]{2,1,0:T(4,128)S(1)} %get-tuple-element.25.refs_5_), channel_id=1, source_target_pairs={{0,12},{4,8},{8,4},{12,0},{1,13},{5,9},{9,5},{13,1},{2,14},{6,10},... | collective-permute-start | bytes 399368 | tf_op jit(solution)/shard_map/ppermute | solution.py:423
  5.3 8.1 %collective-permute-start.1 = (f32[65,4,128]{2,1,0:T(4,128)S(1)}, f32[65,4,128]{2,1,0:T(4,128)S(1)}, u32[]{:S(2)}, u32[]{:S(2)}) collective-permute-start(f32[65,4,128]{2,1,0:T(4,128)S(1)} %get-tuple-element.25.refs_5_), channel_id=1, source_target_pairs={{0,8},{4,12},{8,0},{12,4},{1,9},{5,13},{9,1},{13,5},{2,10},{6,14},... | collective-permute-start | bytes 399368 | tf_op jit(solution)/shard_map/ppermute | solution.py:423
  5.9 7.5 %collective-permute-start = (f32[65,4,128]{2,1,0:T(4,128)S(1)}, f32[65,4,128]{2,1,0:T(4,128)S(1)}, u32[]{:S(2)}, u32[]{:S(2)}) collective-permute-start(f32[65,4,128]{2,1,0:T(4,128)S(1)} %get-tuple-element.25.refs_5_), channel_id=1, source_target_pairs={{0,4},{4,0},{8,12},{12,8},{1,5},{5,1},{9,13},{13,9},{2,6},{6,2},{1... | collective-permute-start | bytes 399368 | tf_op jit(solution)/shard_map/ppermute | solution.py:423
  13.4 18.0 %copy-start = (f32[16384]{0:T(1024)S(1)}, f32[16384]{0:T(1024)}, u32[]{:S(2)}) copy-start(f32[16384]{0:T(1024)} %param.11) | copy-start | bytes 196612
  13.4 18.0 %copy-start.1 = (f32[16384]{0:T(1024)S(1)}, f32[16384]{0:T(1024)}, u32[]{:S(2)}) copy-start(f32[16384]{0:T(1024)} %param.10) | copy-start | bytes 196612
  15.2 6.2 %collective-permute-start.5 = (f32[32,4,128]{2,1,0:T(4,128)S(1)}, f32[32,4,128]{2,1,0:T(4,128)S(1)}, u32[]{:S(2)}, u32[]{:S(2)}) collective-permute-start(f32[32,4,128]{2,1,0:T(4,128)S(1)} %get-tuple-element.29.refs_3_), channel_id=1, source_target_pairs={{0,3},{1,2},{2,1},{3,0},{4,7},{5,6},{6,5},{7,4},{8,11},{9,10},{10,... | collective-permute-start | bytes 196616 | tf_op jit(solution)/shard_map/ppermute | solution.py:423
  17.8 7.7 %collective-permute-start.4 = (f32[32,4,128]{2,1,0:T(4,128)S(1)}, f32[32,4,128]{2,1,0:T(4,128)S(1)}, u32[]{:S(2)}, u32[]{:S(2)}) collective-permute-start(f32[32,4,128]{2,1,0:T(4,128)S(1)} %get-tuple-element.29.refs_3_), channel_id=1, source_target_pairs={{0,2},{1,3},{2,0},{3,1},{4,6},{5,7},{6,4},{7,5},{8,10},{9,11},{10,... | collective-permute-start | bytes 196616 | tf_op jit(solution)/shard_map/ppermute | solution.py:423
  19.8 5.8 %collective-permute-start.3 = (f32[32,4,128]{2,1,0:T(4,128)S(1)}, f32[32,4,128]{2,1,0:T(4,128)S(1)}, u32[]{:S(2)}, u32[]{:S(2)}) collective-permute-start(f32[32,4,128]{2,1,0:T(4,128)S(1)} %get-tuple-element.29.refs_3_), channel_id=1, source_target_pairs={{0,1},{1,0},{2,3},{3,2},{4,5},{5,4},{6,7},{7,6},{8,9},{9,8},{10,11... | collective-permute-start | bytes 196616 | tf_op jit(solution)/shard_map/ppermute | solution.py:423
  27.5 3.2 %collective-permute-start.8 = (f32[9,4,128]{2,1,0:T(4,128)S(1)}, f32[9,4,128]{2,1,0:T(4,128)S(1)}, u32[]{:S(2)}, u32[]{:S(2)}) collective-permute-start(f32[9,4,128]{2,1,0:T(4,128)S(1)} %row_0.1.refs_8_), channel_id=1, source_target_pairs={{0,12},{4,8},{8,4},{12,0},{1,13},{5,9},{9,5},{13,1},{2,14},{6,10},... | collective-permute-start | bytes 55304 | tf_op jit(solution)/shard_map/ppermute | solution.py:423
  27.6 3.8 %collective-permute-start.7 = (f32[9,4,128]{2,1,0:T(4,128)S(1)}, f32[9,4,128]{2,1,0:T(4,128)S(1)}, u32[]{:S(2)}, u32[]{:S(2)}) collective-permute-start(f32[9,4,128]{2,1,0:T(4,128)S(1)} %row_0.1.refs_8_), channel_id=1, source_target_pairs={{0,8},{4,12},{8,0},{12,4},{1,9},{5,13},{9,1},{13,5},{2,10},{6,14},... | collective-permute-start | bytes 55304 | tf_op jit(solution)/shard_map/ppermute | solution.py:423
  27.9 3.5 %collective-permute-start.6 = (f32[9,4,128]{2,1,0:T(4,128)S(1)}, f32[9,4,128]{2,1,0:T(4,128)S(1)}, u32[]{:S(2)}, u32[]{:S(2)}) collective-permute-start(f32[9,4,128]{2,1,0:T(4,128)S(1)} %row_0.1.refs_8_), channel_id=1, source_target_pairs={{0,4},{4,0},{8,12},{12,8},{1,5},{5,1},{9,13},{13,9},{2,6},{6,2},{1... | collective-permute-start | bytes 55304 | tf_op jit(solution)/shard_map/ppermute | solution.py:423
  33.2 6.9 %collective-permute-start.11 = (f32[33,4,128]{2,1,0:T(4,128)S(1)}, f32[33,4,128]{2,1,0:T(4,128)S(1)}, u32[]{:S(2)}, u32[]{:S(2)}) collective-permute-start(f32[33,4,128]{2,1,0:T(4,128)S(1)} %get-tuple-element.32.refs_3_), channel_id=1, source_target_pairs={{0,3},{1,2},{2,1},{3,0},{4,7},{5,6},{6,5},{7,4},{8,11},{9,10},{10,... | collective-permute-start | bytes 202760 | tf_op jit(solution)/shard_map/ppermute | solution.py:423
  33.3 7.2 %collective-permute-start.10 = (f32[33,4,128]{2,1,0:T(4,128)S(1)}, f32[33,4,128]{2,1,0:T(4,128)S(1)}, u32[]{:S(2)}, u32[]{:S(2)}) collective-permute-start(f32[33,4,128]{2,1,0:T(4,128)S(1)} %get-tuple-element.32.refs_3_), channel_id=1, source_target_pairs={{0,2},{1,3},{2,0},{3,1},{4,6},{5,7},{6,4},{7,5},{8,10},{9,11},{10,... | collective-permute-start | bytes 202760 | tf_op jit(solution)/shard_map/ppermute | solution.py:423
  34.5 6.5 %collective-permute-start.9 = (f32[33,4,128]{2,1,0:T(4,128)S(1)}, f32[33,4,128]{2,1,0:T(4,128)S(1)}, u32[]{:S(2)}, u32[]{:S(2)}) collective-permute-start(f32[33,4,128]{2,1,0:T(4,128)S(1)} %get-tuple-element.32.refs_3_), channel_id=1, source_target_pairs={{0,1},{1,0},{2,3},{3,2},{4,5},{5,4},{6,7},{7,6},{8,9},{9,8},{10,11... | collective-permute-start | bytes 202760 | tf_op jit(solution)/shard_map/ppermute | solution.py:423
  43.1 3.2 %collective-permute-start.14 = (f32[9,4,128]{2,1,0:T(4,128)S(1)}, f32[9,4,128]{2,1,0:T(4,128)S(1)}, u32[]{:S(2)}, u32[]{:S(2)}) collective-permute-start(f32[9,4,128]{2,1,0:T(4,128)S(1)} %get-tuple-element.33.refs_9_), channel_id=1, source_target_pairs={{0,12},{4,8},{8,4},{12,0},{1,13},{5,9},{9,5},{13,1},{2,14},{6,10},... | collective-permute-start | bytes 55304 | tf_op jit(solution)/shard_map/ppermute | solution.py:423
  43.1 3.8 %collective-permute-start.13 = (f32[9,4,128]{2,1,0:T(4,128)S(1)}, f32[9,4,128]{2,1,0:T(4,128)S(1)}, u32[]{:S(2)}, u32[]{:S(2)}) collective-permute-start(f32[9,4,128]{2,1,0:T(4,128)S(1)} %get-tuple-element.33.refs_9_), channel_id=1, source_target_pairs={{0,8},{4,12},{8,0},{12,4},{1,9},{5,13},{9,1},{13,5},{2,10},{6,14},... | collective-permute-start | bytes 55304 | tf_op jit(solution)/shard_map/ppermute | solution.py:423
  43.3 3.6 %collective-permute-start.12 = (f32[9,4,128]{2,1,0:T(4,128)S(1)}, f32[9,4,128]{2,1,0:T(4,128)S(1)}, u32[]{:S(2)}, u32[]{:S(2)}) collective-permute-start(f32[9,4,128]{2,1,0:T(4,128)S(1)} %get-tuple-element.33.refs_9_), channel_id=1, source_target_pairs={{0,4},{4,0},{8,12},{12,8},{1,5},{5,1},{9,13},{13,9},{2,6},{6,2},{1... | collective-permute-start | bytes 55304 | tf_op jit(solution)/shard_map/ppermute | solution.py:423
  48.9 6.9 %collective-permute-start.17 = (f32[33,4,128]{2,1,0:T(4,128)S(1)}, f32[33,4,128]{2,1,0:T(4,128)S(1)}, u32[]{:S(2)}, u32[]{:S(2)}) collective-permute-start(f32[33,4,128]{2,1,0:T(4,128)S(1)} %get-tuple-element.38.refs_3_), channel_id=1, source_target_pairs={{0,3},{1,2},{2,1},{3,0},{4,7},{5,6},{6,5},{7,4},{8,11},{9,10},{10,... | collective-permute-start | bytes 202760 | tf_op jit(solution)/shard_map/ppermute | solution.py:423
  49.0 8.4 %collective-permute-start.16 = (f32[33,4,128]{2,1,0:T(4,128)S(1)}, f32[33,4,128]{2,1,0:T(4,128)S(1)}, u32[]{:S(2)}, u32[]{:S(2)}) collective-permute-start(f32[33,4,128]{2,1,0:T(4,128)S(1)} %get-tuple-element.38.refs_3_), channel_id=1, source_target_pairs={{0,2},{1,3},{2,0},{3,1},{4,6},{5,7},{6,4},{7,5},{8,10},{9,11},{10,... | collective-permute-start | bytes 202760 | tf_op jit(solution)/shard_map/ppermute | solution.py:423
  50.9 6.4 %collective-permute-start.15 = (f32[33,4,128]{2,1,0:T(4,128)S(1)}, f32[33,4,128]{2,1,0:T(4,128)S(1)}, u32[]{:S(2)}, u32[]{:S(2)}) collective-permute-start(f32[33,4,128]{2,1,0:T(4,128)S(1)} %get-tuple-element.38.refs_3_), channel_id=1, source_target_pairs={{0,1},{1,0},{2,3},{3,2},{4,5},{5,4},{6,7},{7,6},{8,9},{9,8},{10,11... | collective-permute-start | bytes 202760 | tf_op jit(solution)/shard_map/ppermute | solution.py:423
  59.4 3.2 %collective-permute-start.20 = (f32[9,4,128]{2,1,0:T(4,128)S(1)}, f32[9,4,128]{2,1,0:T(4,128)S(1)}, u32[]{:S(2)}, u32[]{:S(2)}) collective-permute-start(f32[9,4,128]{2,1,0:T(4,128)S(1)} %row_2.1.refs_8_), channel_id=1, source_target_pairs={{0,12},{4,8},{8,4},{12,0},{1,13},{5,9},{9,5},{13,1},{2,14},{6,10},... | collective-permute-start | bytes 55304 | tf_op jit(solution)/shard_map/ppermute | solution.py:423
  59.5 3.8 %collective-permute-start.19 = (f32[9,4,128]{2,1,0:T(4,128)S(1)}, f32[9,4,128]{2,1,0:T(4,128)S(1)}, u32[]{:S(2)}, u32[]{:S(2)}) collective-permute-start(f32[9,4,128]{2,1,0:T(4,128)S(1)} %row_2.1.refs_8_), channel_id=1, source_target_pairs={{0,8},{4,12},{8,0},{12,4},{1,9},{5,13},{9,1},{13,5},{2,10},{6,14},... | collective-permute-start | bytes 55304 | tf_op jit(solution)/shard_map/ppermute | solution.py:423
  59.9 3.4 %collective-permute-start.18 = (f32[9,4,128]{2,1,0:T(4,128)S(1)}, f32[9,4,128]{2,1,0:T(4,128)S(1)}, u32[]{:S(2)}, u32[]{:S(2)}) collective-permute-start(f32[9,4,128]{2,1,0:T(4,128)S(1)} %row_2.1.refs_8_), channel_id=1, source_target_pairs={{0,4},{4,0},{8,12},{12,8},{1,5},{5,1},{9,13},{13,9},{2,6},{6,2},{1... | collective-permute-start | bytes 55304 | tf_op jit(solution)/shard_map/ppermute | solution.py:423

commit v2 on v1

--- a/solution.py
+++ b/solution.py
@@ -68,7 +68,7 @@
     return jnp.sum(jnp.sum(values, axis=0), keepdims=True)
 
 
-def prep_kernel(pairs_in, count, place, x0, damp, payload, table, ids, info, pairs, sems):
+def prep_kernel(pairs_in, place, x0, damp, payload, table, ids, info, pairs, sems):
     own = x0.shape[0]
     slots = ids.shape[0]
     copies = [
@@ -83,7 +83,7 @@
     info[0] = place[0]
     info[1] = place[1]
     pairs_copy.wait()
-    info[2] = count[0, 0]
+    info[2] = place[2]
 
     def assign(i, carry):
         block = pairs[1, i]
@@ -96,7 +96,7 @@
         table[1, i] = slot
         return carry
 
-    lax.fori_loop(0, count[0, 0], assign, 0)
+    lax.fori_loop(0, place[2], assign, 0)
     table[0, pairs.shape[1]] = 0
     table[1, pairs.shape[1]] = 0
     payload[2 * own] = scalar_tile([ids[s].astype(F32) for s in range(slots)])
@@ -125,7 +125,7 @@
     return jnp.concatenate(blocks, axis=0).astype(BF16)
 
 
-def tiles_kernel(table, ids, info, readings, prisms, tiles, rgeo, pgeo, depth, feats, rsems, psems):
+def tiles_kernel(table, ids, info, readings, prisms, tiles, rgeo, pgeo, ups, depth, feats, rsems, psems):
     slots = ids.shape[0]
     count = info[2]
 
@@ -148,14 +148,11 @@
         geo = scaled(pgeo[s])
         feats[s] = features(geo, False).astype(F32)
         for q in range(ROWS):
-            turned = geo[:, q * LANES : (q + 1) * LANES].T
-            for g in range(GROUPS // ROWS):
-                depth[s * GROUPS + q * (GROUPS // ROWS) + g] = jnp.broadcast_to(
-                    turned[8 * g : 8 * g + 8, 2:3], (8, LANES)
-                )
+            ups[s, q : q + 1] = geo[2:3, q * LANES : (q + 1) * LANES]
         return carry
 
     over(slots, prepare)
+    spread_lanes(ups, depth)
     lax.fori_loop(0, count, lambda i, c: (reading_copy(i).wait(), c)[1], 0)
 
     def one(i):
@@ -432,7 +429,7 @@
     slots = n_rd * SLOTS
     shaped = lambda v: v.reshape(-1, ROWS, LANES)
     x0, damp, obs = shaped(warm_start), shaped(damping), shaped(observed)
-    place = jnp.stack([lax.axis_index("rd"), lax.axis_index("pr")]).astype(I32)
+    place = jnp.stack([lax.axis_index("rd"), lax.axis_index("pr"), pair_count[0, 0]]).astype(I32)
     array = lambda *lead: VMEM((*lead, ROWS, LANES), F32)
     wide = VMEM((slots * GROUPS, 8, LANES), F32)
     far = lambda v: pltpu.with_memory_space_constraint(v, HBM)
@@ -444,8 +441,8 @@
         "prep",
         room,
         [array(2 * own + 1), SMEM((2, cap + 1), I32), SMEM((slots,), I32), SMEM((3,), I32)],
-        [HBM, SMEM, SMEM, HBM, HBM],
-        [far(pairs), pair_count, place, far(x0), far(damp)],
+        [HBM, SMEM, HBM, HBM],
+        [far(pairs), place, far(x0), far(damp)],
         [SMEM((2, cap), I32), dma((3,))],
     )
     columns = exchange(payload, "rd", n_rd)
@@ -459,6 +456,7 @@
         [
             VMEM((cap, 8, BLK), F32),
             VMEM((slots, 8, BLK), F32),
+            array(slots),
             wide,
             VMEM((slots, FEATURES, BLK), F32),
             dma((cap,)),

time: 63.9 us -> 62 us (0.970)
  Pallas kernels: 21.5 us -> 11.7 us
  waiting for transfers between devices: 18.7 us -> 23.2 us
  starting transfers between devices: 22.6 us -> 25.5 us
    pallas_call x9, Pallas kernels: 21.5 us -> 11.7 us  [call(): pl.pallas_call(kernel, name=name, out_shape=outs, in_specs=[pl.BlockSpec(...]
    ppermute x21, waiting for transfers between devices: 18.7 us -> 23.2 us  [exchange(): got.append(lax.ppermute(values, axis, pairs))]
    ppermute x21, starting transfers between devices: 22.6 us -> 25.5 us  [exchange(): got.append(lax.ppermute(values, axis, pairs))]
  transfers between devices with their start and end apart: 21 -> 21, of which waited for: 13 -> 14; matrix products, arithmetic and copies ran while one was open for 0% -> 0% of each run, Pallas kernels for 11% -> 5%
where the time goes in v2:
time: 62 us; the launch traced here: 61.9 us
  starting transfers between devices  25.5 us (41%)
  waiting for transfers between devices  23.2 us (37%)
  Pallas kernels  11.7 us (19%)
  between operations  1.39 us (2%)
    ppermute x21, starting transfers between devices, exchange(): got.append(lax.ppermute(values, axis, pairs))  25.5 us
    ppermute x21, waiting for transfers between devices, exchange(): got.append(lax.ppermute(values, axis, pairs))  23.2 us
    pallas_call x9, Pallas kernels, call(): pl.pallas_call(kernel, name=name, out_shape=outs, in_specs=[pl.BlockSpec(...  11.7 us
  transfers between devices with their start and end apart: 21, of which 14 were waited for; matrix products, arithmetic and copies ran while one was open for 0% of the time, Pallas kernels for 5%

profile of v2, /device:TPU:0, one launch (start us, length us, event | category | flops | bytes accessed | tf_op | source)
XLA Modules:
  0.0 61.9 jit_solution(16278399179259802098)
XLA Ops:
  1.4 1.4 %prep.1 = (f32[65,4,128]{2,1,0:T(4,128)S(1)}, s32[2,21]{1,0:T(2,128)S(4)}, s32[8]{0:T(128)S(4)}, s32[3]{0:T(128)S(4)}) custom-call(s32[2,20]{1,0:T(2,128)} %bitcast.20, s32[3]{0:T(128)S(1)} %pad_add_fusion.place, f32[32,4,128]{2,1,0:T(4,128)} %bitcast.16, f32[32,4,128]{2,1,0:T(4,128)} %bitcast.12), custom_call_target="tpu_custom_call" | custom-call | tf_op jit(solution)/shard_map/prep/pallas_call | solution.py:29
  2.8 2.4 %collective-permute-start.2 = (f32[65,4,128]{2,1,0:T(4,128)S(1)}, f32[65,4,128]{2,1,0:T(4,128)S(1)}, u32[]{:S(2)}, u32[]{:S(2)}) collective-permute-start(f32[65,4,128]{2,1,0:T(4,128)S(1)} %get-tuple-element.25.refs_5_), channel_id=1, source_target_pairs={{0,12},{4,8},{8,4},{12,0},{1,13},{5,9},{9,5},{13,1},{2,14},{6,10},... | collective-permute-start | bytes 399368 | tf_op jit(solution)/shard_map/ppermute | solution.py:420
  5.9 2.8 %tiles.1.refs_4_.refs_2_.refs_3_ = f32[1344,8,512]{2,1,0:T(8,128)S(1)} custom-call(s32[2,21]{1,0:T(2,128)S(4)} %get-tuple-element.23.table.refs_0_, s32[8]{0:T(128)S(4)} %get-tuple-element.24.ids.refs_1_, s32[3]{0:T(128)S(4)} %get-tuple-element.22.info.refs_2_.refs_1_.refs_0_, f32[3,16384]{1,0:T(4,128)} %readings.1, f32[3,65536]{1,0:T(4,128)} %prisms.1), custom_call_target="tpu_custom_call" | custom-call | tf_op jit(solution)/shard_map/tiles/pallas_call | solution.py:29
  9.2 3.0 %collective-permute-done.1.refs_7_ = f32[65,4,128]{2,1,0:T(4,128)S(1)} collective-permute-done((f32[65,4,128]{2,1,0:T(4,128)S(1)}, f32[65,4,128]{2,1,0:T(4,128)S(1)}, u32[]{:S(2)}, u32[]{:S(2)}) %collective-permute-start.1) | collective-permute-done | bytes 133152 | tf_op jit(solution)/shard_map/ppermute | solution.py:420
  12.2 1.1 %first_forward.1 = (f32[32,4,128]{2,1,0:T(4,128)S(1)}, f32[8,4,128]{2,1,0:T(4,128)S(1)}, f32[8,4,128]{2,1,0:T(4,128)S(1)}, s32[4,4,128]{2,1,0:T(4,128)S(4)}) custom-call(s32[2,21]{1,0:T(2,128)S(4)} %get-tuple-element.23.table.refs_0_, s32[8]{0:T(128)S(4)} %get-tuple-element.24.ids.refs_1_, s32[3]{0:T(128)S(4)} %get-tuple-element.22.info.refs_2_.refs_1_.refs_0_, ...), custom_call_target="tpu_custom_call" | custom-call | tf_op jit(solution)/shard_map/first_forward/pallas_call | solution.py:29
  13.3 6.2 %collective-permute-start.5 = (f32[32,4,128]{2,1,0:T(4,128)S(1)}, f32[32,4,128]{2,1,0:T(4,128)S(1)}, u32[]{:S(2)}, u32[]{:S(2)}) collective-permute-start(f32[32,4,128]{2,1,0:T(4,128)S(1)} %get-tuple-element.29.refs_3_), channel_id=1, source_target_pairs={{0,3},{1,2},{2,1},{3,0},{4,7},{5,6},{6,5},{7,4},{8,11},{9,10},{10,... | collective-permute-start | bytes 196616 | tf_op jit(solution)/shard_map/ppermute | solution.py:420
  20.2 1.9 %collective-permute-done.5.refs_6_ = f32[32,4,128]{2,1,0:T(4,128)S(1)} collective-permute-done((f32[32,4,128]{2,1,0:T(4,128)S(1)}, f32[32,4,128]{2,1,0:T(4,128)S(1)}, u32[]{:S(2)}, u32[]{:S(2)}) %collective-permute-start.5) | collective-permute-done | bytes 65568 | tf_op jit(solution)/shard_map/ppermute | solution.py:420
  22.1 2.7 %collective-permute-done.4.refs_5_ = f32[32,4,128]{2,1,0:T(4,128)S(1)} collective-permute-done((f32[32,4,128]{2,1,0:T(4,128)S(1)}, f32[32,4,128]{2,1,0:T(4,128)S(1)}, u32[]{:S(2)}, u32[]{:S(2)}) %collective-permute-start.4) | collective-permute-done | bytes 65568 | tf_op jit(solution)/shard_map/ppermute | solution.py:420
  24.8 1.1 %row_0.1.refs_8_ = f32[9,4,128]{2,1,0:T(4,128)S(1)} custom-call(s32[2,21]{1,0:T(2,128)S(4)} %get-tuple-element.23.table.refs_0_, s32[3]{0:T(128)S(4)} %get-tuple-element.22.info.refs_2_.refs_1_.refs_0_, f32[1344,8,512]{2,1,0:T(8,128)S(1)} %tiles.1.refs_4_.refs_2_.refs_3_, f32[32,4,128]{2,1,0:T(4,128)S(1)} %get-tuple-element.29.refs_3_, ...), custom_call_target="tpu_custom_call" | custom-call | tf_op jit(solution)/shard_map/row_0/pallas_call | solution.py:29
  26.5 1.2 %collective-permute-start.6 = (f32[9,4,128]{2,1,0:T(4,128)S(1)}, f32[9,4,128]{2,1,0:T(4,128)S(1)}, u32[]{:S(2)}, u32[]{:S(2)}) collective-permute-start(f32[9,4,128]{2,1,0:T(4,128)S(1)} %row_0.1.refs_8_), channel_id=1, source_target_pairs={{0,4},{4,0},{8,12},{12,8},{1,5},{5,1},{9,13},{13,9},{2,6},{6,2},{1... | collective-permute-start | bytes 55304 | tf_op jit(solution)/shard_map/ppermute | solution.py:420
  27.8 1.3 %collective-permute-done.8.refs_11_ = f32[9,4,128]{2,1,0:T(4,128)S(1)} collective-permute-done((f32[9,4,128]{2,1,0:T(4,128)S(1)}, f32[9,4,128]{2,1,0:T(4,128)S(1)}, u32[]{:S(2)}, u32[]{:S(2)}) %collective-permute-start.8) | collective-permute-done | bytes 18464 | tf_op jit(solution)/shard_map/ppermute | solution.py:420
  30.6 4.2 %collective-permute-start.11 = (f32[33,4,128]{2,1,0:T(4,128)S(1)}, f32[33,4,128]{2,1,0:T(4,128)S(1)}, u32[]{:S(2)}, u32[]{:S(2)}) collective-permute-start(f32[33,4,128]{2,1,0:T(4,128)S(1)} %get-tuple-element.32.refs_3_), channel_id=1, source_target_pairs={{0,3},{1,2},{2,1},{3,0},{4,7},{5,6},{6,5},{7,4},{8,11},{9,10},{10,... | collective-permute-start | bytes 202760 | tf_op jit(solution)/shard_map/ppermute | solution.py:420
  35.4 2.2 %collective-permute-done.11.refs_6_ = f32[33,4,128]{2,1,0:T(4,128)S(1)} collective-permute-done((f32[33,4,128]{2,1,0:T(4,128)S(1)}, f32[33,4,128]{2,1,0:T(4,128)S(1)}, u32[]{:S(2)}, u32[]{:S(2)}) %collective-permute-start.11) | collective-permute-done | bytes 67616 | tf_op jit(solution)/shard_map/ppermute | solution.py:420
  37.6 2.4 %collective-permute-done.10.refs_5_ = f32[33,4,128]{2,1,0:T(4,128)S(1)} collective-permute-done((f32[33,4,128]{2,1,0:T(4,128)S(1)}, f32[33,4,128]{2,1,0:T(4,128)S(1)}, u32[]{:S(2)}, u32[]{:S(2)}) %collective-permute-start.10) | collective-permute-done | bytes 67616 | tf_op jit(solution)/shard_map/ppermute | solution.py:420
  40.0 1.2 %row_1.1 = (f32[9,4,128]{2,1,0:T(4,128)S(1)}, f32[32,4,128]{2,1,0:T(4,128)S(1)}) custom-call(s32[2,21]{1,0:T(2,128)S(4)} %get-tuple-element.23.table.refs_0_, s32[3]{0:T(128)S(4)} %get-tuple-element.22.info.refs_2_.refs_1_.refs_0_, f32[1344,8,512]{2,1,0:T(8,128)S(1)} %tiles.1.refs_4_.refs_2_.refs_3_, f32[33,4,128]{2,1,0:T(4,128)S(1)} %get-tuple-element.32.refs_3_, ...), custom_call_target="tpu_custom_call" | custom-call | tf_op jit(solution)/shard_map/row_1/pallas_call | solution.py:29
  41.7 1.3 %collective-permute-start.12 = (f32[9,4,128]{2,1,0:T(4,128)S(1)}, f32[9,4,128]{2,1,0:T(4,128)S(1)}, u32[]{:S(2)}, u32[]{:S(2)}) collective-permute-start(f32[9,4,128]{2,1,0:T(4,128)S(1)} %get-tuple-element.33.refs_9_), channel_id=1, source_target_pairs={{0,4},{4,0},{8,12},{12,8},{1,5},{5,1},{9,13},{13,9},{2,6},{6,2},{1... | collective-permute-start | bytes 55304 | tf_op jit(solution)/shard_map/ppermute | solution.py:420
  43.1 1.3 %collective-permute-done.14.refs_12_ = f32[9,4,128]{2,1,0:T(4,128)S(1)} collective-permute-done((f32[9,4,128]{2,1,0:T(4,128)S(1)}, f32[9,4,128]{2,1,0:T(4,128)S(1)}, u32[]{:S(2)}, u32[]{:S(2)}) %collective-permute-start.14) | collective-permute-done | bytes 18464 | tf_op jit(solution)/shard_map/ppermute | solution.py:420
  46.2 4.4 %collective-permute-start.17 = (f32[33,4,128]{2,1,0:T(4,128)S(1)}, f32[33,4,128]{2,1,0:T(4,128)S(1)}, u32[]{:S(2)}, u32[]{:S(2)}) collective-permute-start(f32[33,4,128]{2,1,0:T(4,128)S(1)} %get-tuple-element.38.refs_3_), channel_id=1, source_target_pairs={{0,3},{1,2},{2,1},{3,0},{4,7},{5,6},{6,5},{7,4},{8,11},{9,10},{10,... | collective-permute-start | bytes 202760 | tf_op jit(solution)/shard_map/ppermute | solution.py:420
  51.2 1.8 %collective-permute-done.17.refs_6_ = f32[33,4,128]{2,1,0:T(4,128)S(1)} collective-permute-done((f32[33,4,128]{2,1,0:T(4,128)S(1)}, f32[33,4,128]{2,1,0:T(4,128)S(1)}, u32[]{:S(2)}, u32[]{:S(2)}) %collective-permute-start.17) | collective-permute-done | bytes 67616 | tf_op jit(solution)/shard_map/ppermute | solution.py:420
  53.0 2.8 %collective-permute-done.16.refs_5_ = f32[33,4,128]{2,1,0:T(4,128)S(1)} collective-permute-done((f32[33,4,128]{2,1,0:T(4,128)S(1)}, f32[33,4,128]{2,1,0:T(4,128)S(1)}, u32[]{:S(2)}, u32[]{:S(2)}) %collective-permute-start.16) | collective-permute-done | bytes 67616 | tf_op jit(solution)/shard_map/ppermute | solution.py:420
  55.7 1.2 %row_2.1.refs_8_ = f32[9,4,128]{2,1,0:T(4,128)S(1)} custom-call(s32[2,21]{1,0:T(2,128)S(4)} %get-tuple-element.23.table.refs_0_, s32[3]{0:T(128)S(4)} %get-tuple-element.22.info.refs_2_.refs_1_.refs_0_, f32[1344,8,512]{2,1,0:T(8,128)S(1)} %tiles.1.refs_4_.refs_2_.refs_3_, f32[33,4,128]{2,1,0:T(4,128)S(1)} %get-tuple-element.38.refs_3_, ...), custom_call_target="tpu_custom_call" | custom-call | tf_op jit(solution)/shard_map/row_2/pallas_call | solution.py:29
  57.1 1.7 %collective-permute-start.18 = (f32[9,4,128]{2,1,0:T(4,128)S(1)}, f32[9,4,128]{2,1,0:T(4,128)S(1)}, u32[]{:S(2)}, u32[]{:S(2)}) collective-permute-start(f32[9,4,128]{2,1,0:T(4,128)S(1)} %row_2.1.refs_8_), channel_id=1, source_target_pairs={{0,4},{4,0},{8,12},{12,8},{1,5},{5,1},{9,13},{13,9},{2,6},{6,2},{1... | collective-permute-start | bytes 55304 | tf_op jit(solution)/shard_map/ppermute | solution.py:420
  58.8 1.3 %collective-permute-done.20.refs_11_ = f32[9,4,128]{2,1,0:T(4,128)S(1)} collective-permute-done((f32[9,4,128]{2,1,0:T(4,128)S(1)}, f32[9,4,128]{2,1,0:T(4,128)S(1)}, u32[]{:S(2)}, u32[]{:S(2)}) %collective-permute-start.20) | collective-permute-done | bytes 18464 | tf_op jit(solution)/shard_map/ppermute | solution.py:420
  60.8 1.1 %last.1 = (f32[32,4,128]{2,1,0:T(4,128)}, f32[32,4,128]{2,1,0:T(4,128)}) custom-call(s32[3]{0:T(128)S(4)} %get-tuple-element.22.info.refs_2_.refs_1_.refs_0_, s32[4,4,128]{2,1,0:T(4,128)S(4)} %get-tuple-element.26.refs_2_.refs_1_, f32[32,4,128]{2,1,0:T(4,128)S(1)} %bitcast.15, f32[32,4,128]{2,1,0:T(4,128)S(1)} %get-tuple-element.34.refs_3_, ...), custom_call_target="tpu_custom_call" | custom-call | tf_op jit(solution)/shard_map/last/pallas_call | solution.py:29
  (34 shorter events, 8.5 us)
Async XLA Ops:
  0.6 11.6 %copy-start.2 = (f32[4096]{0:T(1024)S(1)}, f32[4096]{0:T(1024)}, u32[]{:S(2)}) copy-start(f32[4096]{0:T(1024)} %param.9) | copy-start | bytes 49156
  2.8 6.4 %collective-permute-start.2 = (f32[65,4,128]{2,1,0:T(4,128)S(1)}, f32[65,4,128]{2,1,0:T(4,128)S(1)}, u32[]{:S(2)}, u32[]{:S(2)}) collective-permute-start(f32[65,4,128]{2,1,0:T(4,128)S(1)} %get-tuple-element.25.refs_5_), channel_id=1, source_target_pairs={{0,12},{4,8},{8,4},{12,0},{1,13},{5,9},{9,5},{13,1},{2,14},{6,10},... | collective-permute-start | bytes 399368 | tf_op jit(solution)/shard_map/ppermute | solution.py:420
  5.3 7.0 %collective-permute-start.1 = (f32[65,4,128]{2,1,0:T(4,128)S(1)}, f32[65,4,128]{2,1,0:T(4,128)S(1)}, u32[]{:S(2)}, u32[]{:S(2)}) collective-permute-start(f32[65,4,128]{2,1,0:T(4,128)S(1)} %get-tuple-element.25.refs_5_), channel_id=1, source_target_pairs={{0,8},{4,12},{8,0},{12,4},{1,9},{5,13},{9,1},{13,5},{2,10},{6,14},... | collective-permute-start | bytes 399368 | tf_op jit(solution)/shard_map/ppermute | solution.py:420
  5.9 6.3 %collective-permute-start = (f32[65,4,128]{2,1,0:T(4,128)S(1)}, f32[65,4,128]{2,1,0:T(4,128)S(1)}, u32[]{:S(2)}, u32[]{:S(2)}) collective-permute-start(f32[65,4,128]{2,1,0:T(4,128)S(1)} %get-tuple-element.25.refs_5_), channel_id=1, source_target_pairs={{0,4},{4,0},{8,12},{12,8},{1,5},{5,1},{9,13},{13,9},{2,6},{6,2},{1... | collective-permute-start | bytes 399368 | tf_op jit(solution)/shard_map/ppermute | solution.py:420
  12.2 17.5 %copy-start = (f32[16384]{0:T(1024)S(1)}, f32[16384]{0:T(1024)}, u32[]{:S(2)}) copy-start(f32[16384]{0:T(1024)} %param.11) | copy-start | bytes 196612
  12.2 17.5 %copy-start.1 = (f32[16384]{0:T(1024)S(1)}, f32[16384]{0:T(1024)}, u32[]{:S(2)}) copy-start(f32[16384]{0:T(1024)} %param.10) | copy-start | bytes 196612
  13.3 8.7 %collective-permute-start.5 = (f32[32,4,128]{2,1,0:T(4,128)S(1)}, f32[32,4,128]{2,1,0:T(4,128)S(1)}, u32[]{:S(2)}, u32[]{:S(2)}) collective-permute-start(f32[32,4,128]{2,1,0:T(4,128)S(1)} %get-tuple-element.29.refs_3_), channel_id=1, source_target_pairs={{0,3},{1,2},{2,1},{3,0},{4,7},{5,6},{6,5},{7,4},{8,11},{9,10},{10,... | collective-permute-start | bytes 196616 | tf_op jit(solution)/shard_map/ppermute | solution.py:420
  19.6 5.2 %collective-permute-start.4 = (f32[32,4,128]{2,1,0:T(4,128)S(1)}, f32[32,4,128]{2,1,0:T(4,128)S(1)}, u32[]{:S(2)}, u32[]{:S(2)}) collective-permute-start(f32[32,4,128]{2,1,0:T(4,128)S(1)} %get-tuple-element.29.refs_3_), channel_id=1, source_target_pairs={{0,2},{1,3},{2,0},{3,1},{4,6},{5,7},{6,4},{7,5},{8,10},{9,11},{10,... | collective-permute-start | bytes 196616 | tf_op jit(solution)/shard_map/ppermute | solution.py:420
  19.6 5.2 %collective-permute-start.3 = (f32[32,4,128]{2,1,0:T(4,128)S(1)}, f32[32,4,128]{2,1,0:T(4,128)S(1)}, u32[]{:S(2)}, u32[]{:S(2)}) collective-permute-start(f32[32,4,128]{2,1,0:T(4,128)S(1)} %get-tuple-element.29.refs_3_), channel_id=1, source_target_pairs={{0,1},{1,0},{2,3},{3,2},{4,5},{5,4},{6,7},{7,6},{8,9},{9,8},{10,11... | collective-permute-start | bytes 196616 | tf_op jit(solution)/shard_map/ppermute | solution.py:420
  25.9 3.2 %collective-permute-start.8 = (f32[9,4,128]{2,1,0:T(4,128)S(1)}, f32[9,4,128]{2,1,0:T(4,128)S(1)}, u32[]{:S(2)}, u32[]{:S(2)}) collective-permute-start(f32[9,4,128]{2,1,0:T(4,128)S(1)} %row_0.1.refs_8_), channel_id=1, source_target_pairs={{0,12},{4,8},{8,4},{12,0},{1,13},{5,9},{9,5},{13,1},{2,14},{6,10},... | collective-permute-start | bytes 55304 | tf_op jit(solution)/shard_map/ppermute | solution.py:420
  25.9 3.8 %collective-permute-start.7 = (f32[9,4,128]{2,1,0:T(4,128)S(1)}, f32[9,4,128]{2,1,0:T(4,128)S(1)}, u32[]{:S(2)}, u32[]{:S(2)}) collective-permute-start(f32[9,4,128]{2,1,0:T(4,128)S(1)} %row_0.1.refs_8_), channel_id=1, source_target_pairs={{0,8},{4,12},{8,0},{12,4},{1,9},{5,13},{9,1},{13,5},{2,10},{6,14},... | collective-permute-start | bytes 55304 | tf_op jit(solution)/shard_map/ppermute | solution.py:420
  26.5 3.2 %collective-permute-start.6 = (f32[9,4,128]{2,1,0:T(4,128)S(1)}, f32[9,4,128]{2,1,0:T(4,128)S(1)}, u32[]{:S(2)}, u32[]{:S(2)}) collective-permute-start(f32[9,4,128]{2,1,0:T(4,128)S(1)} %row_0.1.refs_8_), channel_id=1, source_target_pairs={{0,4},{4,0},{8,12},{12,8},{1,5},{5,1},{9,13},{13,9},{2,6},{6,2},{1... | collective-permute-start | bytes 55304 | tf_op jit(solution)/shard_map/ppermute | solution.py:420
  30.6 7.0 %collective-permute-start.11 = (f32[33,4,128]{2,1,0:T(4,128)S(1)}, f32[33,4,128]{2,1,0:T(4,128)S(1)}, u32[]{:S(2)}, u32[]{:S(2)}) collective-permute-start(f32[33,4,128]{2,1,0:T(4,128)S(1)} %get-tuple-element.32.refs_3_), channel_id=1, source_target_pairs={{0,3},{1,2},{2,1},{3,0},{4,7},{5,6},{6,5},{7,4},{8,11},{9,10},{10,... | collective-permute-start | bytes 202760 | tf_op jit(solution)/shard_map/ppermute | solution.py:420
  34.8 5.2 %collective-permute-start.10 = (f32[33,4,128]{2,1,0:T(4,128)S(1)}, f32[33,4,128]{2,1,0:T(4,128)S(1)}, u32[]{:S(2)}, u32[]{:S(2)}) collective-permute-start(f32[33,4,128]{2,1,0:T(4,128)S(1)} %get-tuple-element.32.refs_3_), channel_id=1, source_target_pairs={{0,2},{1,3},{2,0},{3,1},{4,6},{5,7},{6,4},{7,5},{8,10},{9,11},{10,... | collective-permute-start | bytes 202760 | tf_op jit(solution)/shard_map/ppermute | solution.py:420
  34.8 5.2 %collective-permute-start.9 = (f32[33,4,128]{2,1,0:T(4,128)S(1)}, f32[33,4,128]{2,1,0:T(4,128)S(1)}, u32[]{:S(2)}, u32[]{:S(2)}) collective-permute-start(f32[33,4,128]{2,1,0:T(4,128)S(1)} %get-tuple-element.32.refs_3_), channel_id=1, source_target_pairs={{0,1},{1,0},{2,3},{3,2},{4,5},{5,4},{6,7},{7,6},{8,9},{9,8},{10,11... | collective-permute-start | bytes 202760 | tf_op jit(solution)/shard_map/ppermute | solution.py:420
  41.2 3.2 %collective-permute-start.14 = (f32[9,4,128]{2,1,0:T(4,128)S(1)}, f32[9,4,128]{2,1,0:T(4,128)S(1)}, u32[]{:S(2)}, u32[]{:S(2)}) collective-permute-start(f32[9,4,128]{2,1,0:T(4,128)S(1)} %get-tuple-element.33.refs_9_), channel_id=1, source_target_pairs={{0,12},{4,8},{8,4},{12,0},{1,13},{5,9},{9,5},{13,1},{2,14},{6,10},... | collective-permute-start | bytes 55304 | tf_op jit(solution)/shard_map/ppermute | solution.py:420
  41.4 3.8 %collective-permute-start.13 = (f32[9,4,128]{2,1,0:T(4,128)S(1)}, f32[9,4,128]{2,1,0:T(4,128)S(1)}, u32[]{:S(2)}, u32[]{:S(2)}) collective-permute-start(f32[9,4,128]{2,1,0:T(4,128)S(1)} %get-tuple-element.33.refs_9_), channel_id=1, source_target_pairs={{0,8},{4,12},{8,0},{12,4},{1,9},{5,13},{9,1},{13,5},{2,10},{6,14},... | collective-permute-start | bytes 55304 | tf_op jit(solution)/shard_map/ppermute | solution.py:420
  41.7 3.4 %collective-permute-start.12 = (f32[9,4,128]{2,1,0:T(4,128)S(1)}, f32[9,4,128]{2,1,0:T(4,128)S(1)}, u32[]{:S(2)}, u32[]{:S(2)}) collective-permute-start(f32[9,4,128]{2,1,0:T(4,128)S(1)} %get-tuple-element.33.refs_9_), channel_id=1, source_target_pairs={{0,4},{4,0},{8,12},{12,8},{1,5},{5,1},{9,13},{13,9},{2,6},{6,2},{1... | collective-permute-start | bytes 55304 | tf_op jit(solution)/shard_map/ppermute | solution.py:420
  46.2 6.8 %collective-permute-start.17 = (f32[33,4,128]{2,1,0:T(4,128)S(1)}, f32[33,4,128]{2,1,0:T(4,128)S(1)}, u32[]{:S(2)}, u32[]{:S(2)}) collective-permute-start(f32[33,4,128]{2,1,0:T(4,128)S(1)} %get-tuple-element.38.refs_3_), channel_id=1, source_target_pairs={{0,3},{1,2},{2,1},{3,0},{4,7},{5,6},{6,5},{7,4},{8,11},{9,10},{10,... | collective-permute-start | bytes 202760 | tf_op jit(solution)/shard_map/ppermute | solution.py:420
  50.6 5.2 %collective-permute-start.16 = (f32[33,4,128]{2,1,0:T(4,128)S(1)}, f32[33,4,128]{2,1,0:T(4,128)S(1)}, u32[]{:S(2)}, u32[]{:S(2)}) collective-permute-start(f32[33,4,128]{2,1,0:T(4,128)S(1)} %get-tuple-element.38.refs_3_), channel_id=1, source_target_pairs={{0,2},{1,3},{2,0},{3,1},{4,6},{5,7},{6,4},{7,5},{8,10},{9,11},{10,... | collective-permute-start | bytes 202760 | tf_op jit(solution)/shard_map/ppermute | solution.py:420
  50.6 5.2 %collective-permute-start.15 = (f32[33,4,128]{2,1,0:T(4,128)S(1)}, f32[33,4,128]{2,1,0:T(4,128)S(1)}, u32[]{:S(2)}, u32[]{:S(2)}) collective-permute-start(f32[33,4,128]{2,1,0:T(4,128)S(1)} %get-tuple-element.38.refs_3_), channel_id=1, source_target_pairs={{0,1},{1,0},{2,3},{3,2},{4,5},{5,4},{6,7},{7,6},{8,9},{9,8},{10,11... | collective-permute-start | bytes 202760 | tf_op jit(solution)/shard_map/ppermute | solution.py:420
  56.9 3.2 %collective-permute-start.20 = (f32[9,4,128]{2,1,0:T(4,128)S(1)}, f32[9,4,128]{2,1,0:T(4,128)S(1)}, u32[]{:S(2)}, u32[]{:S(2)}) collective-permute-start(f32[9,4,128]{2,1,0:T(4,128)S(1)} %row_2.1.refs_8_), channel_id=1, source_target_pairs={{0,12},{4,8},{8,4},{12,0},{1,13},{5,9},{9,5},{13,1},{2,14},{6,10},... | collective-permute-start | bytes 55304 | tf_op jit(solution)/shard_map/ppermute | solution.py:420
  57.0 3.8 %collective-permute-start.19 = (f32[9,4,128]{2,1,0:T(4,128)S(1)}, f32[9,4,128]{2,1,0:T(4,128)S(1)}, u32[]{:S(2)}, u32[]{:S(2)}) collective-permute-start(f32[9,4,128]{2,1,0:T(4,128)S(1)} %row_2.1.refs_8_), channel_id=1, source_target_pairs={{0,8},{4,12},{8,0},{12,4},{1,9},{5,13},{9,1},{13,5},{2,10},{6,14},... | collective-permute-start | bytes 55304 | tf_op jit(solution)/shard_map/ppermute | solution.py:420
  57.1 3.7 %collective-permute-start.18 = (f32[9,4,128]{2,1,0:T(4,128)S(1)}, f32[9,4,128]{2,1,0:T(4,128)S(1)}, u32[]{:S(2)}, u32[]{:S(2)}) collective-permute-start(f32[9,4,128]{2,1,0:T(4,128)S(1)} %row_2.1.refs_8_), channel_id=1, source_target_pairs={{0,4},{4,0},{8,12},{12,8},{1,5},{5,1},{9,13},{13,9},{2,6},{6,2},{1... | collective-permute-start | bytes 55304 | tf_op jit(solution)/shard_map/ppermute | solution.py:420
